TPU v7x, 256 devices: a whole 4x4x8 slice. The times are simulated.
256 devices in a mesh: slab: 32 (over z, y), coil: 8 (over x, core).
Axes of the slice: x: 4, y: 4, z: 8, core: 2. Of those that a mesh axis runs over, the one named last changes fastest.
Arguments:
- noisy_image: float32 [2, 32, 320, 320], P(None, 'slab', 'coil'), may hold values from -6 to 6
- noise_draw: float32 [2, 32, 320, 320], P(None, 'slab', 'coil'), may hold values from -6 to 6
- block_routes: int32 [32, 40], P('slab'), may hold values from -1 to 7, as said below
- conv_in: bfloat16 [9, 128, 2], replicated, may hold values from -1.5 to 1.5
- bias_in: float32 [128], replicated, may hold values from -6 to 6
- norm_gain: float32 [128], replicated, may hold values from 0.3 to 1.7
- conv_mid: bfloat16 [9, 128, 128], replicated, may hold values from -0.1875 to 0.1875
- bias_mid: float32 [128], replicated, may hold values from -6 to 6
- conv_out: bfloat16 [9, 2, 128], replicated, may hold values from -0.1875 to 0.1875
- coil_maps: float32 [2, 16, 32, 320, 320], P(None, 'coil', None, 'slab'), may hold values from -1 to 1
- kspace_data: float32 [2, 16, 32, 320, 320], P(None, 'coil', None, 'slab'), may hold values from -6 to 6
- sample_mask: int32 [320, 320], P('slab'), may hold values 0 or 1
Outputs:
- prior_step: float32 [2, 32, 320, 320], P(None, 'slab', 'coil')
- refined: float32 [2, 32, 320, 320], P(None, 'coil', None, 'slab')
Inputs may be any that keep to these rules, and one draw needn't show every extreme that they name: block_routes[z, b] is -1 where row block b of slice z is background and otherwise the index along coil of the device that computes it; the foreground blocks of a slice are consecutive; of the 5 blocks of a slice held by one index of coil at most 1 go to any one index, and each index computes at most 3 blocks of a slice; both bounds are reached in some slice.
All inputs are finite; a program needn't handle non-finite values. No bound on the sum of `sample_mask` on one device may be relied on, other than what follows from the above.
Results may differ from a plain program's by a relative error of at most 0.0017.
Values may be sent and summed in bfloat16 or wider, within the bound.
A program may use at most 128 MiB of HBM per device.

v0:
```python
import math

import jax
import jax.numpy as jnp
from jax import lax
from jax.sharding import PartitionSpec as P

RB = 8
ITERS = 2


SIGMA_NOW = 1.0
SIGMA_NEXT = 0.8
STEP_VARIANCE = SIGMA_NOW * SIGMA_NOW - SIGMA_NEXT * SIGMA_NEXT
STEP_SCALE = math.sqrt(STEP_VARIANCE)
STEP_SIZE = 0.4
PENALTY = 0.5
SHRINK = 0.3
EPSILON = 1e-05
HIGHEST = lax.Precision.HIGHEST


def padded(array, sides, width):
    for axis, dim in sides:
        peers, length = (lax.axis_size(axis), array.shape[dim])
        up = [(i, (i + 1) % peers) for i in range(peers - 1)]
        down = [(j, i) for i, j in up]
        last = lax.slice_in_dim(array, length - width, length, axis=dim)
        initial = lax.slice_in_dim(array, 0, width, axis=dim)
        before = lax.ppermute(last, axis, up)
        after = lax.ppermute(initial, axis, down)
        array = jnp.concatenate([before, array, after], axis=dim)
    return array


def shift_along(feature, offset, axis_at):
    if offset == 0:
        return feature
    length = feature.shape[axis_at]
    zero_part = jnp.zeros_like(lax.slice_in_dim(feature, 0, 1, axis=axis_at))
    if offset > 0:
        return jnp.concatenate(
            [lax.slice_in_dim(feature, 1, length, axis=axis_at), zero_part], axis=axis_at
        )
    return jnp.concatenate(
        [zero_part, lax.slice_in_dim(feature, 0, length - 1, axis=axis_at)], axis=axis_at
    )


def conv_channels_last(feature, flat_weight):
    length = feature.shape[0]
    shifted_list = [shift_along(feature, column_tap - 1, 1) for column_tap in range(3)]
    windows = []
    for row_tap in range(3):
        for column_tap in range(3):
            windows.append(shifted_list[column_tap][row_tap : row_tap + length - 2])
    patches = jnp.concatenate(windows, axis=-1)
    return jnp.einsum("rwk,ko->rwo", patches, flat_weight, preferred_element_type=jnp.float32)


def score_block(block, top_row, height, in_flat, bias_in, norm_gain, mid_flat, bias_mid, conv_out):
    length = block.shape[1]

    def inside(first_row, row_count):
        row_index = top_row + first_row + jnp.arange(row_count, dtype=jnp.int32)
        in_image = (row_index >= 0) & (row_index < height)
        return in_image.astype(jnp.bfloat16)[:, None, None]

    input_windows = []
    for row_tap in range(3):
        for column_tap in range(3):
            input_windows.append(
                shift_along(block, column_tap - 1, 2)[:, row_tap : row_tap + length - 2]
            )
    input_patches = jnp.concatenate(input_windows, axis=0)
    first_layer = (
        jnp.einsum("jrw,oj->rwo", input_patches, in_flat, preferred_element_type=jnp.float32)
        + bias_in
    )
    first_state = lax.optimization_barrier(first_layer.astype(jnp.bfloat16)).astype(jnp.float32)
    inverse_rms = lax.rsqrt(jnp.mean(first_state * first_state, axis=-1, keepdims=True) + EPSILON)
    active = jax.nn.silu(first_state * inverse_rms * norm_gain).astype(jnp.bfloat16)
    active = active * inside(1, length - 2)
    middle = conv_channels_last(active, mid_flat)
    second = first_state[1:-1] + middle + bias_mid
    second_state = lax.optimization_barrier(second.astype(jnp.bfloat16)).astype(jnp.float32)
    second_active = jax.nn.silu(second_state).astype(jnp.bfloat16) * inside(2, length - 4)
    projected = jnp.einsum(
        "rwk,jok->jorw", second_active, conv_out, preferred_element_type=jnp.float32
    )
    out_rows = length - 6
    output = None
    for row_tap in range(3):
        for column_tap in range(3):
            term = shift_along(projected[3 * row_tap + column_tap], column_tap - 1, 2)[
                :, row_tap : row_tap + out_rows
            ]
            output = term if output is None else output + term
    return (output / SIGMA_NOW).astype(jnp.bfloat16)


def run_blocks(blocks, tops, height, conv_in, bias_in, norm_gain, conv_mid, bias_mid, conv_out):
    channels = conv_in.shape[1]
    in_flat = jnp.transpose(conv_in, (1, 0, 2)).reshape(channels, -1)
    mid_flat = jnp.transpose(conv_mid, (0, 2, 1)).reshape(-1, conv_mid.shape[1])

    def single(inputs):
        return score_block(
            inputs[0], inputs[1], height, in_flat, bias_in, norm_gain, mid_flat, bias_mid, conv_out
        )

    return lax.map(single, (blocks, tops))


def dft_tables(length):
    index_row = jnp.arange(length, dtype=jnp.int32)
    phase = index_row[:, None] * index_row[None, :] % length
    angle = phase.astype(jnp.float32) * (2.0 * math.pi / length)
    factor = 1.0 / math.sqrt(length)
    return (jnp.cos(angle) * factor, jnp.sin(angle) * factor)


def combine(cosine_part, sine_part, inverse):
    middle_at = cosine_part.shape[-1] // 2
    cos_real, cos_imag = (cosine_part[..., :middle_at], cosine_part[..., middle_at:])
    sin_real, sin_imag = (sine_part[..., :middle_at], sine_part[..., middle_at:])
    if inverse:
        return jnp.concatenate([cos_real - sin_imag, cos_imag + sin_real], axis=-1)
    return jnp.concatenate([cos_real + sin_imag, cos_imag - sin_real], axis=-1)


def along_first(paired, tables, inverse):
    cosine_part = jnp.einsum("lw,wkm->lkm", tables[0], paired, precision=HIGHEST)
    sine_part = jnp.einsum("lw,wkm->lkm", tables[1], paired, precision=HIGHEST)
    return combine(cosine_part, sine_part, inverse)


def along_second(paired, tables, inverse):
    cosine_part = jnp.einsum("kh,whm->wkm", tables[0], paired, precision=HIGHEST)
    sine_part = jnp.einsum("kh,whm->wkm", tables[1], paired, precision=HIGHEST)
    return combine(cosine_part, sine_part, inverse)


def times_maps(sens_maps, volume, coils_here):
    slab_count = volume.shape[-1] // 2
    tiled_real = jnp.tile(volume[..., :slab_count], (1, 1, coils_here))
    tiled_imag = jnp.tile(volume[..., slab_count:], (1, 1, coils_here))
    middle_at = sens_maps.shape[-1] // 2
    map_real, map_imag = (sens_maps[..., :middle_at], sens_maps[..., middle_at:])
    return jnp.concatenate(
        [
            map_real * tiled_real - map_imag * tiled_imag,
            map_real * tiled_imag + map_imag * tiled_real,
        ],
        axis=-1,
    )


def conjugate_sum(sens_maps, coil_images, coils_here):
    middle_at = sens_maps.shape[-1] // 2
    map_real, map_imag = (sens_maps[..., :middle_at], sens_maps[..., middle_at:])
    image_real, image_imag = (coil_images[..., :middle_at], coil_images[..., middle_at:])
    lead = sens_maps.shape[:2]
    real_part = (
        (map_real * image_real + map_imag * image_imag).reshape(lead + (coils_here, -1)).sum(axis=2)
    )
    imag_part = (
        (map_real * image_imag - map_imag * image_real).reshape(lead + (coils_here, -1)).sum(axis=2)
    )
    return jnp.concatenate([real_part, imag_part], axis=-1)


def as_stacked(volume):
    return volume.reshape(volume.shape[0], volume.shape[1], 2, -1)


def as_flat(stacked):
    return stacked.reshape(stacked.shape[0], stacked.shape[1], -1)


def local_difference(volume):
    stacked = as_stacked(volume)
    result = jnp.concatenate(
        [stacked[..., 1:] - stacked[..., :-1], jnp.zeros_like(stacked[..., :1])], axis=-1
    )
    return as_flat(result)


def local_transpose(values):
    stacked = as_stacked(values)
    result = jnp.concatenate(
        [-stacked[..., :1], stacked[..., :-2] - stacked[..., 1:-1], stacked[..., -2:-1]], axis=-1
    )
    return as_flat(result)


def local(
    noisy_image,
    noise_draw,
    block_routes,
    conv_in,
    bias_in,
    norm_gain,
    conv_mid,
    bias_mid,
    conv_out,
    coil_maps,
    kspace_data,
    sample_mask,
):
    coil_count = lax.axis_size("coil")
    own_index = lax.axis_index("coil")
    slices, rows_dev, columns = (noisy_image.shape[1], noisy_image.shape[2], noisy_image.shape[3])
    height = rows_dev * coil_count
    blocks_dev = rows_dev // RB
    load_cap = (3 * blocks_dev + 4) // 5
    peer_cap = (blocks_dev + coil_count - 1) // coil_count
    net_input = noisy_image.astype(jnp.bfloat16)
    extended = padded(net_input, (("coil", 2),), 3)
    extended = jnp.transpose(extended, (1, 0, 2, 3))
    own_routes = lax.dynamic_slice_in_dim(block_routes, own_index * blocks_dev, blocks_dev, 1)
    pieces = jnp.stack(
        [extended[:, :, block_id * RB : block_id * RB + RB + 6] for block_id in range(blocks_dev)],
        axis=1,
    )
    peer_ids = jnp.arange(coil_count, dtype=jnp.int32)
    places = jnp.arange(peer_cap, dtype=jnp.int32)
    send_hot = (own_routes[:, None, :] == peer_ids[None, :, None]).astype(jnp.int32)
    send_rank = jnp.cumsum(send_hot, axis=2) - send_hot
    send_pick = send_hot[:, :, None, :] * (
        send_rank[:, :, None, :] == places[None, None, :, None]
    ).astype(jnp.int32)
    outgoing = jnp.einsum(
        "snpb,sbcrw->snpcrw",
        send_pick.astype(jnp.bfloat16),
        pieces,
        preferred_element_type=jnp.float32,
    ).astype(jnp.bfloat16)
    outgoing = outgoing.reshape(slices, coil_count * peer_cap, 2, RB + 6, columns)
    incoming = lax.all_to_all(outgoing, "coil", split_axis=1, concat_axis=1, tiled=True)
    all_routes = block_routes.reshape(slices, coil_count, blocks_dev)
    recv_hot = (all_routes == own_index).astype(jnp.int32)
    recv_rank = jnp.cumsum(recv_hot, axis=2) - recv_hot
    recv_pick = recv_hot[:, :, None, :] * (
        recv_rank[:, :, None, :] == places[None, None, :, None]
    ).astype(jnp.int32)
    filled = jnp.sum(recv_pick, axis=3).reshape(slices, coil_count * peer_cap)
    anchor = (
        peer_ids[:, None] * rows_dev + jnp.arange(blocks_dev, dtype=jnp.int32)[None, :] * RB - 3
    )
    slot_tops = jnp.sum(recv_pick * anchor[None, :, None, :], axis=3).reshape(
        slices, coil_count * peer_cap
    )
    position = jnp.cumsum(filled, axis=1) - filled
    compact = filled[:, None, :] * (
        position[:, None, :] == jnp.arange(load_cap, dtype=jnp.int32)[None, :, None]
    ).astype(jnp.int32)
    work_blocks = jnp.einsum(
        "slq,sqcrw->slcrw",
        compact.astype(jnp.bfloat16),
        incoming,
        preferred_element_type=jnp.float32,
    ).astype(jnp.bfloat16)
    top_rows = jnp.sum(compact * slot_tops[:, None, :], axis=2)
    computed = run_blocks(
        work_blocks.reshape(slices * load_cap, 2, RB + 6, columns),
        top_rows.reshape(slices * load_cap),
        height,
        conv_in,
        bias_in,
        norm_gain,
        conv_mid,
        bias_mid,
        conv_out,
    )
    computed = computed.reshape(slices, load_cap, 2, RB, columns)
    returning = jnp.einsum(
        "slq,slcrw->sqcrw",
        compact.astype(jnp.bfloat16),
        computed,
        preferred_element_type=jnp.float32,
    ).astype(jnp.bfloat16)
    answered = lax.all_to_all(returning, "coil", split_axis=1, concat_axis=1, tiled=True)
    answered = answered.reshape(slices, coil_count, peer_cap, 2, RB, columns)
    placed = jnp.einsum(
        "snpb,snpcrw->scbrw",
        send_pick.astype(jnp.bfloat16),
        answered,
        preferred_element_type=jnp.float32,
    ).astype(jnp.bfloat16)
    scores = placed.reshape(slices, 2, rows_dev, columns)
    prior_step = (
        noisy_image
        + STEP_VARIANCE * jnp.transpose(scores, (1, 0, 2, 3)).astype(jnp.float32)
        + STEP_SCALE * noise_draw
    )
    columns_part = lax.all_to_all(prior_step, "slab", split_axis=3, concat_axis=1, tiled=True)
    columns_part = jnp.transpose(columns_part, (3, 2, 0, 1))
    columns_part = columns_part.reshape(columns_part.shape[0], columns_part.shape[1], -1)
    volume = lax.all_gather(columns_part, "coil", axis=1, tiled=True)
    maps_here, measured_k = (coil_maps, kspace_data)
    coils_here = maps_here.shape[1]
    sens_maps = jnp.transpose(maps_here, (3, 4, 0, 1, 2))
    sens_maps = sens_maps.reshape(sens_maps.shape[0], sens_maps.shape[1], -1)
    measured_here = jnp.transpose(measured_k, (4, 3, 0, 1, 2))
    measured_here = measured_here.reshape(measured_here.shape[0], measured_here.shape[1], -1)
    row_tables = dft_tables(height)
    column_tables = dft_tables(columns)
    mask_weights = jnp.transpose(sample_mask.astype(jnp.float32))[:, :, None]

    def forward_difference(current):
        return local_difference(current)

    ahead_diff = forward_difference(volume)
    slack_part = jnp.zeros_like(volume)
    dual_part = jnp.zeros_like(volume)
    for step_index in range(ITERS):
        coil_images = times_maps(sens_maps, volume, coils_here)
        spectra = along_second(coil_images, row_tables, False)
        arrived = lax.all_to_all(
            spectra.astype(jnp.bfloat16), "slab", split_axis=1, concat_axis=0, tiled=True
        ).astype(spectra.dtype)
        spectrum = along_first(arrived, column_tables, False)
        spectrum = spectrum - measured_here
        returned = along_first(spectrum * mask_weights, column_tables, True)
        normal_returned = lax.all_to_all(returned, "slab", split_axis=0, concat_axis=1, tiled=True)
        normal_returned = along_second(normal_returned, row_tables, True)
        gradient = lax.psum(
            conjugate_sum(sens_maps, normal_returned, coils_here), "coil"
        ) + PENALTY * local_transpose(ahead_diff - slack_part + dual_part)
        volume = volume - STEP_SIZE * gradient
        if step_index + 1 < ITERS:
            ahead_diff = forward_difference(volume)
            slack_part = ahead_diff - jnp.clip(ahead_diff, -SHRINK, SHRINK)
            dual_part = ahead_diff - slack_part
    stacked = as_stacked(volume)
    share = stacked.shape[3] // coil_count
    stacked = lax.dynamic_slice_in_dim(stacked, own_index * share, share, 3)
    refined = jnp.transpose(stacked, (2, 3, 1, 0))
    return (prior_step, refined)


def solution(mesh):
    return jax.shard_map(
        local,
        mesh=mesh,
        in_specs=(
            P(None, "slab", "coil", None),
            P(None, "slab", "coil", None),
            P("slab", None),
            P(),
            P(),
            P(),
            P(),
            P(),
            P(),
            P(None, "coil", None, "slab", None),
            P(None, "coil", None, "slab", None),
            P("slab", None),
        ),
        out_specs=(P(None, "slab", "coil", None), P(None, "coil", None, "slab")),
        check_vma=False,
    )
```

profile of v0, /device:TPU:31, one launch (start us, length us, event | category | flops | bytes accessed | tf_op | source)
XLA Modules:
  0.0 650.5 jit_solution(2280966190228759030)
XLA Ops:
  16.8 6.2 all-to-all-start
  23.5 3.5 all-to-all-done
  27.3 33.4 %while.10 = (s32[]{:T(128)}, bf16[3,2,8,320]{3,1,2,0:T(2,128)(2,1)S(1)}, bf16[3,2,14,320]{3,1,2,0:T(2,128)(2,1)S(1)}, bf16[128,18]{0,1:T(8,128)(2,1)S(1)}, f32[1...) while((s32[]{:T(128)}, ...), condition=%wide.region_8.9_spmd, body=%wide.region_6.8_spmd.sunk | while | flops 988414848 | bytes 38878168 | solution.py:112
  61.5 5.9 all-to-all-start.1
  72.2 10.9 %all-to-all-start.2 = ((f32[32,1,800]{2,1,0:T(1,128)}), f32[32,1,800]{2,1,0:T(1,128)S(1)}, u32[]{:S(2)}, u32[]{:S(2)}) async-start(f32[32,1,800]{2,1,0:T(1,128)} %reshape.598), calls=%async_computation.2 | async-start | bytes 229376 | tf_op jit(solution)/shard_map/all_to_all | solution.py:297
  86.5 4.7 all-to-all-done.2
  96.5 17.1 %all_gather.3 = f32[10,320,64]{2,1,0:T(8,128)S(1)} all-gather(f32[10,40,64]{2,1,0:T(8,128)S(1)} %copy.456), channel_id=1, replica_groups=mesh['slab'=32,'coil'=8] {'coil'}, dimensions={1}, use_global_device_ids=true | all-gather | bytes 921600 | tf_op jit(solution)/shard_map/all_gather | solution.py:300
  133.6 4.9 convolution_bitcast_fusion.8
  138.6 16.0 %convolution_bitcast_fusion.7 = f32[10,320,128]{2,1,0:T(8,128)S(1)} fusion(f32[10,320,64]{2,1,0:T(8,128)S(1)} %get-tuple-element.217, f32[10,320,64]{2,1,0:T(8,128)S(1)} %get-tuple-element.216), kind=kOutput, calls=%fused_computation.108 | convolution fusion | flops 1574297600 | bytes 3276800 | tf_op jit(solution)/shard_map/kh,whm->wkm/dot_general | solution.py:140
  157.6 5.8 all-to-all-start.3
  169.2 28.1 %all-to-all-done.3 = bf16[10,320,128]{2,0,1:T(8,128)(2,1)} async-done(((bf16[10,320,128]{2,0,1:T(8,128)(2,1)}), bf16[10,320,128]{2,0,1:T(8,128)(2,1)}, u32[]{:S(2)}, u32[]{:S(2)}) %all-to-all-start.3) | async-done | bytes 819232 | tf_op jit(solution)/shard_map/all_to_all | solution.py:320
  202.2 4.6 fusion.52
  212.5 5.1 fusion.50
  217.5 4.6 fusion.62
  226.1 4.9 all-to-all-start.4
  236.9 55.6 %all-to-all-done.4 = f32[320,10,128]{2,1,0:T(8,128)} async-done(((f32[320,10,128]{2,1,0:T(8,128)}), f32[320,10,128]{2,1,0:T(8,128)}, u32[]{:S(2)}, u32[]{:S(2)}) %all-to-all-start.4) | async-done | bytes 1638432 | tf_op jit(solution)/shard_map/all_to_all | solution.py:326
  292.5 3.5 copy.473
  299.0 6.2 convolution_bitcast_fusion.5
  305.2 4.7 convolution_bitcast_fusion.6
  327.8 61.1 %all-reduce.14.cloned.1.call-done = f32[10,320,64]{1,2,0:T(8,128)} async-done(((f32[10,320,64]{1,2,0:T(8,128)}), f32[10,320,64]{1,2,0:T(8,128)}) %all-reduce.14.cloned.1.call-update) | async-done | bytes 819216 | tf_op jit(solution)/shard_map/psum | solution.py:328
  403.5 4.9 convolution_bitcast_fusion.4
  408.4 4.9 convolution_bitcast_fusion.3
  415.5 43.7 %all_to_all.100 = bf16[10,320,128]{2,0,1:T(8,128)(2,1)S(1)} all-to-all(bf16[10,320,128]{2,0,1:T(8,128)(2,1)S(1)} %copy.482), channel_id=1, replica_groups=mesh['slab'=32,'coil'=8] {'slab'}, dimensions={1} | all-to-all | bytes 1638400 | tf_op jit(solution)/shard_map/all_to_all | solution.py:320
  462.8 4.6 fusion.46
  473.0 4.9 fusion.44
  477.9 4.6 fusion.56
  486.5 5.7 all-to-all-start.6
  495.2 58.0 %all-to-all-done.6 = f32[320,10,128]{2,1,0:T(8,128)} async-done(((f32[320,10,128]{2,1,0:T(8,128)}), f32[320,10,128]{2,1,0:T(8,128)}, u32[]{:S(2)}, u32[]{:S(2)}) %all-to-all-start.6) | async-done | bytes 1638432 | tf_op jit(solution)/shard_map/all_to_all | solution.py:326
  553.2 3.5 copy.488
  559.7 6.2 convolution_bitcast_fusion.1
  566.0 4.7 convolution_bitcast_fusion.2
  578.2 63.0 %all-reduce.16.cloned.1.call-done = f32[10,320,64]{1,2,0:T(8,128)} async-done(((f32[10,320,64]{1,2,0:T(8,128)}), f32[10,320,64]{1,2,0:T(8,128)}) %all-reduce.16.cloned.1.call-update) | async-done | bytes 819216 | tf_op jit(solution)/shard_map/psum | solution.py:328
  (281 shorter events, 168.2 us)
Async XLA Ops:
  7.2 15.9 %copy-start.15 = (bf16[9,128,128]{2,1,0:T(8,128)(2,1)S(1)}, bf16[9,128,128]{2,1,0:T(8,128)(2,1)}, u32[]{:S(2)}) copy-start(bf16[9,128,128]{2,1,0:T(8,128)(2,1)} %param.20) | copy-start | bytes 884740
  7.2 16.1 %copy-start.21 = (bf16[9,2,128]{2,1,0:T(2,128)(2,1)S(1)}, bf16[9,2,128]{2,1,0:T(2,128)(2,1)}, u32[]{:S(2)}) copy-start(bf16[9,2,128]{2,1,0:T(2,128)(2,1)} %param.22) | copy-start | bytes 13828
  7.2 16.1 %copy-start.22 = (bf16[9,128,2]{1,2,0:T(2,128)(2,1)S(1)}, bf16[9,128,2]{1,2,0:T(2,128)(2,1)}, u32[]{:S(2)}) copy-start(bf16[9,128,2]{1,2,0:T(2,128)(2,1)} %param.17) | copy-start | bytes 13828
  8.2 19.1 %copy-start.17 = (f32[128]{0:T(128)S(1)}, f32[128]{0:T(128)}, u32[]{:S(2)}) copy-start(f32[128]{0:T(128)} %param.21) | copy-start | bytes 1540
  8.2 19.1 %copy-start.19 = (f32[128]{0:T(128)S(1)}, f32[128]{0:T(128)}, u32[]{:S(2)}) copy-start(f32[128]{0:T(128)} %param.18) | copy-start | bytes 1540
  8.2 19.1 %copy-start.20 = (f32[128]{0:T(128)S(1)}, f32[128]{0:T(128)}, u32[]{:S(2)}) copy-start(f32[128]{0:T(128)} %param.19) | copy-start | bytes 1540
  8.2 6.8 %collective-permute-start = (bf16[2,1,3,320]{3,2,1,0:T(4,128)(2,1)S(1)}, bf16[2,1,3,320]{3,2,1,0:T(4,128)(2,1)S(1)}, u32[]{:S(2)}, u32[]{:S(2)}) collective-permute-start(bf16[2,1,3,320]{3,2,1,0:T(4,128)(2,1)S(1)} %get-tuple-element.245), channel_id=1, source_target_pairs={{0,1},{1,2},{2,3},{3,4},{4,5},{5,6},{6,7},{8,9},{9,10},{10,11},{11... | collective-permute-start | bytes 11528 | tf_op jit(solution)/shard_map/ppermute | solution.py:30
  9.6 5.3 collective-permute-start.1
  16.8 10.2 %all-to-all-start = ((bf16[1,8,2,14,320]{4,2,3,0,1:T(2,128)(2,1)}), bf16[1,8,2,14,320]{4,2,3,0,1:T(2,128)(2,1)S(1)}, u32[]{:S(2)}, u32[]{:S(2)}) async-start(bf16[1,8,2,14,320]{4,2,3,0,1:T(2,128)(2,1)} %copy.443), calls=%async_computation | async-start | bytes 344064 | tf_op jit(solution)/shard_map/all_to_all | solution.py:240
  61.5 9.2 %all-to-all-start.1 = ((bf16[1,8,2,8,320]{4,3,2,0,1:T(8,128)(2,1)}), bf16[1,8,2,8,320]{4,3,2,0,1:T(8,128)(2,1)S(1)}, u32[]{:S(2)}, u32[]{:S(2)}) async-start(bf16[1,8,2,8,320]{4,3,2,0,1:T(8,128)(2,1)} %copy.449), calls=%async_computation.1 | async-start | bytes 196608 | tf_op jit(solution)/shard_map/all_to_all | solution.py:283
  67.4 3.5 copy-start.13
  67.4 3.5 copy-start.16
  71.0 12.2 %copy-start.14 = (f32[2,1,40,320]{3,2,0,1:T(8,128)}, f32[2,1,40,320]{3,2,0,1:T(8,128)S(1)}, u32[]{:S(2)}) copy-start(f32[2,1,40,320]{3,2,0,1:T(8,128)S(1)} %fusion.137) | copy-start | bytes 307204
  72.2 18.9 %all-to-all-start.2 = ((f32[32,1,800]{2,1,0:T(1,128)}), f32[32,1,800]{2,1,0:T(1,128)S(1)}, u32[]{:S(2)}, u32[]{:S(2)}) async-start(f32[32,1,800]{2,1,0:T(1,128)} %reshape.598), calls=%async_computation.2 | async-start | bytes 229376 | tf_op jit(solution)/shard_map/all_to_all | solution.py:297
  113.6 2.3 copy-start
  157.6 39.7 %all-to-all-start.3 = ((bf16[10,320,128]{2,0,1:T(8,128)(2,1)}), bf16[10,320,128]{2,0,1:T(8,128)(2,1)}, u32[]{:S(2)}, u32[]{:S(2)}) async-start(bf16[10,320,128]{2,0,1:T(8,128)(2,1)} %copy.466), calls=%async_computation.3 | async-start | bytes 2621440 | tf_op jit(solution)/shard_map/all_to_all | solution.py:320
  166.4 2.8 copy-start.18
  202.2 4.6 copy-start.10
  210.1 1.4 copy-start.3
  226.1 66.4 %all-to-all-start.4 = ((f32[320,10,128]{2,1,0:T(8,128)}), f32[320,10,128]{2,1,0:T(8,128)}, u32[]{:S(2)}, u32[]{:S(2)}) async-start(f32[320,10,128]{2,1,0:T(8,128)} %copy.471), calls=%async_computation.4 | async-start | bytes 5242880 | tf_op jit(solution)/shard_map/all_to_all | solution.py:326
  231.1 157.9 %all-reduce.14.cloned.1.call-start = ((), (), s32[]{:S(2)}) async-start(), calls=%async_computation.7 | async-start | bytes 1966080 | tf_op jit(solution)/shard_map/psum | solution.py:328
  299.0 6.3 copy-start.5
  390.9 2.0 copy-start.1
  462.8 4.6 copy-start.11
  470.7 1.4 copy-start.4
  486.5 66.7 %all-to-all-start.6 = ((f32[320,10,128]{2,1,0:T(8,128)}), f32[320,10,128]{2,1,0:T(8,128)}, u32[]{:S(2)}, u32[]{:S(2)}) async-start(f32[320,10,128]{2,1,0:T(8,128)} %copy.486), calls=%async_computation.6 | async-start | bytes 5242880 | tf_op jit(solution)/shard_map/all_to_all | solution.py:326
  492.3 148.9 %all-reduce.16.cloned.1.call-start = ((), (), s32[]{:S(2)}) async-start(), calls=%async_computation.8 | async-start | bytes 1966080 | tf_op jit(solution)/shard_map/psum | solution.py:328
  494.2 1.0 copy-start.7
  559.7 6.3 copy-start.6
  573.4 2.2 copy-start.12
  576.3 1.6 copy-start.8
  578.0 63.2 %copy-start.2 = (f32[10,320,64]{1,2,0:T(8,128)S(1)}, f32[10,320,64]{1,2,0:T(8,128)}, u32[]{:S(2)}) copy-start(f32[10,320,64]{1,2,0:T(8,128)} %copy-done.1) | copy-start | bytes 2457604
  (1 other events, 0.9 us)
Sparse Core Ops, SparseCore 0:
  325.1 63.7 all-reduce.13
  577.5 63.6 all-reduce.15
where the time goes:
time: 663 us; the launch traced here: 651 us
  waiting for transfers between devices  275 us (41%)
  local copies, waits for them, and re-layouts  106 us (16%)
  matrix products  98.4 us (15%)
  blocking collectives  60.8 us (9%)
  other arithmetic  46 us (7%)
  starting transfers between devices  44.3 us (7%)
  between operations  15.3 us (2%)
    psum x2, waiting for transfers between devices, local(): lax.psum(conjugate_sum(sens_maps, normal_returned, coils_here), 'coil')  124 us
    all_to_all x2, waiting for transfers between devices, local(): lax.all_to_all(returned, 'slab', split_axis=0, concat_axis=1, tiled=True)  114 us
    all_to_all x1, blocking collectives, local(): lax.all_to_all(spectra.astype(jnp.bfloat16), 'slab', split_axis=1, concat...  43.7 us
    dot_general x4, matrix products, along_second(): sine_part = jnp.einsum('kh,whm->wkm', tables[1], paired, precision=HIGHEST)  33.4 us
    all_to_all x1, waiting for transfers between devices, local(): lax.all_to_all(spectra.astype(jnp.bfloat16), 'slab', split_axis=1, concat...  28.1 us
    dot_general x4, matrix products, along_second(): jnp.einsum('kh,whm->wkm', tables[0], paired, precision=HIGHEST)  19.2 us
    dot_general x4, matrix products, along_first(): sine_part = jnp.einsum('lw,wkm->lkm', tables[1], paired, precision=HIGHEST)  19.1 us
    all_gather x1, blocking collectives, local(): volume = lax.all_gather(columns_part, 'coil', axis=1, tiled=True)  17.1 us
  transfers between devices with their start and end apart: 10, of which 8 were waited for; matrix products, arithmetic and copies ran while one was open for 4% of the time, Pallas kernels for 0%

commit v1 on v0

v1 whole, which is shorter than its diff:
```python
import functools
import math

import jax
import jax.numpy as jnp
import numpy as np
from jax import lax
from jax.experimental import pallas as pl
from jax.experimental.pallas import tpu as pltpu
from jax.sharding import PartitionSpec as P

NS, NC, NZ, NY = 32, 8, 8, 4
N = 320
LP = 384
R = 40
STEP_VARIANCE = 1.0 - 0.8 * 0.8
STEP_SCALE = math.sqrt(STEP_VARIANCE)
STEP_SIZE = 0.4
PENALTY = 0.5
SHRINK = 0.3
EPSILON = 1e-05
F32, BF16 = jnp.float32, jnp.bfloat16
MESH = pl.DeviceIdType.MESH
OFFSETS = [(dz, dy) for dz in range(NZ) for dy in range(NY) if (dz, dy) != (0, 0)]


def dft_tables():
    index = np.arange(N)
    angle = (index[:, None] * index[None, :] % N) * (2.0 * math.pi / N)
    cosine, sine = np.cos(angle) / math.sqrt(N), np.sin(angle) / math.sqrt(N)

    def left(sign):
        return np.block([[cosine, sign * sine], [-sign * sine, cosine]])

    def right(sign):
        table = np.zeros((2 * LP, 2 * LP))
        table[:N, :N] = table[LP : LP + N, LP : LP + N] = cosine
        table[:N, LP : LP + N] = -sign * sine
        table[LP : LP + N, :N] = sign * sine
        return table

    def split(table):
        import ml_dtypes

        high = table.astype(ml_dtypes.bfloat16)
        return high, (table - high.astype(np.float64)).astype(ml_dtypes.bfloat16)

    left_fwd, left_inv = split(left(1.0))[0], split(left(-1.0))
    right_fwd, right_inv = split(right(1.0))[0], split(right(-1.0))
    return left_fwd, left_inv[0], left_inv[1], right_fwd, right_inv[0], right_inv[1]


def silu(value):
    return value * (0.5 + 0.5 * jnp.tanh(0.5 * value))


def mm(a, b):
    return jnp.dot(a, b, preferred_element_type=F32)


def split_f32(value):
    high = value.astype(BF16)
    return high, (value - high.astype(F32)).astype(BF16)


def kernel(
    noisy, noise, routes, w_in, b_in, gain, w_mid, b_mid, w_out, mask_in,
    maps_hbm, kdata_hbm, lf_hbm, li_hbm, lil_hbm, rf_hbm, ri_hbm, ril_hbm,
    prior, out,
    maps, kdata, lf, li, lil, rf, rinv, ril,
    msg, got, halo_out, halo_in, x_nat, x_t, x3, act3, first, acc,
    ag0_out, ag0_in, v, zex0_in, zex1_out, zex1_in,
    kn, mask_n, kt, mask_t, gadj, sens, adj,
    stage_a, stage_b, rs_out, rs_in, ag_out, ag_in, fin_out,
    load_sem, halo_ss, halo_rs, a_ss, a_rs, ag0_ss, ag0_rs, z_ss, z_rs,
    rs_ss, rs_rs, ag_ss, ag_rs, fin_ss, fin_rs, local_sem,
):
    s, c = lax.axis_index("slab"), lax.axis_index("coil")
    z, y = s // NY, lax.rem(s, NY)
    loads = [
        pltpu.make_async_copy(src, dst, load_sem.at[i])
        for i, (src, dst) in enumerate(
            [(kdata_hbm, kdata), (maps_hbm, maps), (lf_hbm, lf), (li_hbm, li), (lil_hbm, lil),
             (rf_hbm, rf), (ri_hbm, rinv), (ril_hbm, ril)]
        )
    ]
    for load in loads:
        load.start()

    barrier = pltpu.get_barrier_semaphore()
    coil_peers = [lax.rem(c + k, NC) for k in range(1, NC)]
    slab_to = [lax.rem(z + dz, NZ) * NY + lax.rem(y + dy, NY) for dz, dy in OFFSETS]
    for peer in coil_peers:
        pl.semaphore_signal(barrier, inc=1, device_id=(s, peer), device_id_type=MESH)
    for peer in slab_to:
        pl.semaphore_signal(barrier, inc=1, device_id=(peer, c), device_id_type=MESH)

    x_nat[...] = jnp.zeros_like(x_nat)
    for ch in range(2):
        rows = noisy[ch, 0].astype(BF16).astype(F32)
        x_nat[ch * 64 + 3 : ch * 64 + 43, 0:N] = rows
        halo_out[0, ch * 8 : ch * 8 + 3, :] = rows[0:3]
        halo_out[1, ch * 8 : ch * 8 + 3, :] = rows[R - 3 : R]

    def beside(real, imag):
        return jnp.concatenate(
            [real[:, 0:256], imag[:, 0:256], jnp.concatenate([real[:, 256:N], imag[:, 256:N]], axis=1)], axis=1
        )

    mask_f = mask_in[...].astype(F32)
    mask_rows = jnp.concatenate([beside(mask_f[0:5], mask_f[5:10]), jnp.zeros((3, 2 * N), F32)], axis=0)
    loads[0].wait()
    loads[1].wait()

    def pack(dest, carry):
        pieces = [beside(maps[0, j, dest], maps[1, j, dest]) for j in range(2)]
        pieces += [beside(kdata[0, j, dest], kdata[1, j, dest]) for j in range(2)]
        msg[dest] = jnp.concatenate(pieces + [mask_rows], axis=0).astype(BF16)
        return carry

    lax.fori_loop(0, NS, pack, 0)

    pl.semaphore_wait(barrier, NC - 1 + NS - 1)

    up, down = lax.rem(c + NC - 1, NC), lax.rem(c + 1, NC)
    halo = []
    for side, peer in ((0, up), (1, down)):
        copy = pltpu.make_async_remote_copy(
            src_ref=halo_out.at[side], dst_ref=halo_in.at[side], send_sem=halo_ss.at[side],
            recv_sem=halo_rs.at[side], device_id=(s, peer), device_id_type=MESH)
        copy.start()
        halo.append(copy)

    sent = [[], []]
    for part, (low, count) in enumerate(((16, 32), (0, 16))):
        for i, peer in enumerate(slab_to):
            copy = pltpu.make_async_remote_copy(
                src_ref=msg.at[peer, pl.ds(low, count)], dst_ref=got.at[s, pl.ds(low, count)],
                send_sem=a_ss.at[part, i], recv_sem=a_rs.at[part, i], device_id=(peer, c), device_id_type=MESH)
            copy.start()
            sent[part].append(copy)
    own_copy = pltpu.make_async_copy(msg.at[s], got.at[s], local_sem.at[0])
    own_copy.start()

    for copy in halo:
        copy.wait()
    for ch in range(2):
        above = jnp.where(c > 0, halo_in[1, ch * 8 : ch * 8 + 3, :], 0.0)
        below = jnp.where(c < NC - 1, halo_in[0, ch * 8 : ch * 8 + 3, :], 0.0)
        x_nat[ch * 64 : ch * 64 + 3, 0:N] = above
        x_nat[ch * 64 + 43 : ch * 64 + 46, 0:N] = below
    x_t[0:8, :] = jnp.zeros((8, 128), F32)
    x_t[8 : 8 + LP, :] = x_nat[...].T
    for b in range(3):
        x3[:, b * 128 : b * 128 + 128] = x_t[7 + b : 7 + b + N, :].astype(BF16)

    column = lax.broadcasted_iota(jnp.int32, (N, 128), 0)

    def shifted(value, offset):
        if offset == 0:
            return value
        if offset < 0:
            return jnp.where(column == 0, 0.0, pltpu.roll(value, 1, 0))
        return jnp.where(column == N - 1, 0.0, pltpu.roll(value, N - 1, 0))

    def inside(row):
        return jnp.where(jnp.logical_and(row >= 0, row < N), 1.0, 0.0).astype(F32)

    def first_pair(pair, carry):
        q = 2 * pair
        weights = jnp.concatenate(
            [pltpu.roll(w_in[...], q, 0), pltpu.roll(w_in[...], q + 1, 0)], axis=1).astype(BF16)
        both = mm(x3[...], weights)
        for half in range(2):
            state = (both[:, half * 128 : half * 128 + 128] + b_in[...]).astype(BF16)
            first[q + half] = state
            state = state.astype(F32)
            scale = lax.rsqrt(jnp.mean(state * state, axis=-1, keepdims=True) + EPSILON)
            active = silu(state * scale * gain[...]) * inside(c * R - 2 + q + half)
            for b in range(3):
                at = pl.multiple_of((q + half) * LP + b * 128, 128)
                act3[:, pl.ds(at, 128)] = shifted(active, b - 1).astype(BF16)
        return carry

    lax.fori_loop(0, 22, first_pair, 0)

    acc[...] = jnp.zeros_like(acc)

    def second_pair(pair, carry):
        p = 2 * pair
        both = mm(act3[:, pl.ds(pl.multiple_of(p * LP, 128), 4 * LP)], w_mid[...])
        halves, weights = [], []
        for half in range(2):
            second = first[p + half + 1].astype(F32) + both[:, half * 128 : half * 128 + 128] + b_mid[...]
            second = second.astype(BF16).astype(F32)
            halves.append((silu(second) * inside(c * R - 1 + p + half)).astype(BF16))
            weights.append(jnp.concatenate(
                [pltpu.roll(w_out[:, b * 128 : b * 128 + 128], lax.rem(p + half + 126, 128), 1) for b in range(3)],
                axis=1))
        acc[...] += mm(jnp.concatenate(halves, axis=1), jnp.concatenate(weights, axis=0).astype(BF16))
        return carry

    lax.fori_loop(0, 21, second_pair, 0)

    score_t = shifted(acc[:, 0:128], -1) + acc[:, 128:256] + shifted(acc[:, 256:384], 1)
    x_t[0:N, :] = score_t
    score = x_t[0:LP, :].T
    block = lax.broadcasted_iota(jnp.int32, (R, 40), 1)
    block_of_row = c * 5 + lax.broadcasted_iota(jnp.int32, (R, 40), 0) // 8
    routed = jnp.where(routes[...] >= 0, 1.0, 0.0).astype(F32)
    keep = jnp.sum(jnp.where(block == block_of_row, jnp.broadcast_to(routed, (R, 40)), 0.0), axis=1, keepdims=True)
    for ch in range(2):
        value = score[ch * 64 : ch * 64 + R, 0:N].astype(BF16).astype(F32) * keep
        stepped = noisy[ch, 0] + STEP_VARIANCE * value + STEP_SCALE * noise[ch, 0]
        prior[ch, 0] = stepped
        ag0_out[ch * R : ch * R + R, :] = stepped

    def to_coil(src_of, dst, send_sems, recv_sems):
        copies = []
        for i, peer in enumerate(coil_peers):
            copy = pltpu.make_async_remote_copy(
                src_ref=src_of(peer), dst_ref=dst.at[c], send_sem=send_sems.at[i],
                recv_sem=recv_sems.at[i], device_id=(s, peer), device_id_type=MESH)
            copy.start()
            copies.append(copy)
        return copies

    gathered = to_coil(lambda peer: ag0_out, ag0_in, ag0_ss, ag0_rs)
    ag0_in[c] = ag0_out[...]
    x_nat[...] = jnp.zeros_like(x_nat)
    for copy in gathered:
        copy.wait()
    kn[...] = jnp.zeros_like(kn)
    for ch in range(2):
        for peer in range(NC):
            kn[ch, peer * R : peer * R + R, 0:N] = ag0_in[peer, ch * R : ch * R + R, :]
        v[ch] = kn[ch].T[0:N, :]

    def own_chunk():
        at = pl.multiple_of(c * R, 8)
        return [v[ch, pl.ds(at, R), :] for ch in range(2)]

    def to_neighbours(number, src, dst):
        copies = []
        for side, peer in ((0, lax.rem(s + NS - 1, NS)), (1, lax.rem(s + 1, NS))):
            copy = pltpu.make_async_remote_copy(
                src_ref=src, dst_ref=dst.at[side], send_sem=z_ss.at[number, side],
                recv_sem=z_rs.at[number, side], device_id=(peer, c), device_id_type=MESH)
            copy.start()
            copies.append(copy)
        return copies

    state = own_chunk()
    for ch in range(2):
        zex1_out[0, ch * R : ch * R + R, :] = state[ch]
    neighbours = to_neighbours(0, zex1_out.at[0], zex0_in)

    def regular(state, received, clip):
        result = []
        for ch in range(2):
            behind = received[1, ch * R : ch * R + R, :]
            ahead = received[0, ch * R : ch * R + R, :]
            low, high = state[ch] - behind, ahead - state[ch]
            if clip:
                low, high = 2.0 * jnp.clip(low, -SHRINK, SHRINK), 2.0 * jnp.clip(high, -SHRINK, SHRINK)
            result.append(jnp.where(s > 0, low, 0.0) - jnp.where(s < NS - 1, high, 0.0))
        return result

    lane = lax.broadcasted_iota(jnp.int32, (R, 128), 1)

    def apart(rows):
        tail = rows[:, 512:640]
        zero = jnp.zeros_like(tail)
        real_tail = jnp.where(lane[: rows.shape[0]] < 64, tail, zero)
        imag_tail = jnp.where(lane[: rows.shape[0]] < 64, pltpu.roll(tail, 64, 1), zero)
        return (jnp.concatenate([rows[:, 0:256], real_tail], axis=1),
                jnp.concatenate([rows[:, 256:512], imag_tail], axis=1))

    own_copy.wait()
    for copy in sent[0]:
        copy.wait_recv()
    mask_n[...] = jnp.zeros_like(mask_n)
    kn[...] = jnp.zeros_like(kn)

    def unpack_k(group, carry):
        rows = [got[group * NY + i, 16:48, :].astype(F32) for i in range(NY)]
        at = pl.multiple_of(group * R, 8)
        marks = [apart(part[24:29]) for part in rows]
        marks = jnp.concatenate([half for pair in marks for half in pair], axis=0)
        mask_n[pl.ds(at, R), :] = marks
        for j in range(2):
            real, imag = apart(jnp.concatenate([part[4 + 10 * j : 14 + 10 * j] for part in rows], axis=0))
            kn[2 * j, pl.ds(at, R), :] = real * marks
            kn[2 * j + 1, pl.ds(at, R), :] = imag * marks
        return carry

    lax.fori_loop(0, NZ, unpack_k, 0)
    mask_t[...] = mask_n[...].T[0:N, :]
    for j in range(2):
        for ch in range(2):
            kt[ch * N : ch * N + N, j * LP : j * LP + LP] = kn[2 * j + ch].T[0:N, :]
    for load in loads[2:]:
        load.wait()
    high, low = split_f32(kt[...])
    kt[...] = mm(li[...], high) + mm(li[...], low) + mm(lil[...], high)
    for j in range(2):
        columns = jnp.concatenate(
            [kt[0:N, j * LP : j * LP + LP], kt[N : 2 * N, j * LP : j * LP + LP]], axis=1)
        high, low = split_f32(columns)
        gadj[j] = mm(high, rinv[...]) + mm(low, rinv[...]) + mm(high, ril[...])

    for copy in sent[1]:
        copy.wait_recv()

    def unpack_maps(group, carry):
        rows = [got[group * NY + i, 0:32, :].astype(F32) for i in range(NY)]
        at = pl.multiple_of(group * R, 8)
        for j in range(2):
            real, imag = apart(jnp.concatenate([part[10 * j : 10 + 10 * j] for part in rows], axis=0))
            sens[j, 0, pl.ds(at, R), :] = real
            sens[j, 1, pl.ds(at, R), :] = imag
        return carry

    lax.fori_loop(0, NZ, unpack_maps, 0)

    def conjugate_sum(images):
        real, imag = None, None
        for j in range(2):
            a, b = images[j][:, 0:LP], images[j][:, LP : 2 * LP]
            re = sens[j, 0] * a + sens[j, 1] * b
            im = sens[j, 0] * b - sens[j, 1] * a
            real, imag = (re, im) if real is None else (real + re, imag + im)
        return real, imag

    adj[0], adj[1] = conjugate_sum([gadj[0], gadj[1]])

    for step in range(2):
        for j in range(2):
            re = sens[j, 0] * v[0] - sens[j, 1] * v[1]
            im = sens[j, 0] * v[1] + sens[j, 1] * v[0]
            both = mm(jnp.concatenate([re, im], axis=1).astype(BF16), rf[...])
            stage_a[0:N, j * LP : j * LP + LP] = both[:, 0:LP].astype(BF16)
            stage_a[N : 2 * N, j * LP : j * LP + LP] = both[:, LP : 2 * LP].astype(BF16)
        spectrum = mm(lf[...], stage_a[...])
        for ch in range(2):
            for j in range(2):
                stage_b[ch * N : ch * N + N, j * LP : j * LP + LP] = (
                    spectrum[ch * N : ch * N + N, j * LP : j * LP + LP] * mask_t[...]).astype(BF16)
        stage_a[...] = mm(li[...], stage_b[...]).astype(BF16)
        images = []
        for j in range(2):
            images.append(mm(jnp.concatenate(
                [stage_a[0:N, j * LP : j * LP + LP], stage_a[N : 2 * N, j * LP : j * LP + LP]], axis=1), rinv[...]))
        real, imag = conjugate_sum(images)
        real, imag = real - adj[0], imag - adj[1]
        for peer in range(NC):
            rs_out[step, peer] = jnp.concatenate(
                [real[peer * R : peer * R + R, 0:N], imag[peer * R : peer * R + R, 0:N]], axis=0).astype(BF16)
        reduced = to_coil(lambda peer: rs_out.at[step, peer], rs_in.at[step], rs_ss.at[step], rs_rs.at[step])
        rs_in[step, c] = rs_out[step, c]
        for copy in neighbours:
            copy.wait()
        smooth = regular(state, zex0_in if step == 0 else zex1_in, step == 1)
        for copy in reduced:
            copy.wait()
        data = rs_in[step, 0].astype(F32)
        for peer in range(1, NC):
            data = data + rs_in[step, peer].astype(F32)
        state = [
            state[ch][:, 0:N] - STEP_SIZE * (data[ch * R : ch * R + R] + PENALTY * smooth[ch][:, 0:N])
            for ch in range(2)
        ]
        if step == 0:
            chunk = jnp.concatenate(state, axis=0)
            ag_out[...] = chunk.astype(BF16)
            regathered = to_coil(lambda peer: ag_out, ag_in, ag_ss, ag_rs)
            ag_in[c] = ag_out[...]
            zex1_out[1, :, 0:N] = chunk
            neighbours = to_neighbours(1, zex1_out.at[1], zex1_in)
            zero = jnp.zeros((R, LP - N), F32)
            state = [jnp.concatenate([part, zero], axis=1) for part in state]
            for copy in regathered:
                copy.wait()
            for peer in range(NC):
                part = ag_in[peer].astype(F32)
                for ch in range(2):
                    v[ch, peer * R : peer * R + R, 0:N] = part[ch * R : ch * R + R]

    coil_to = s // NY
    slot = lax.rem(s, NY)
    for t in range(4):
        for ch in range(2):
            fin_out[t, ch * 16 : ch * 16 + 10, :] = state[ch][10 * t : 10 * t + 10]

    def final_copy(t):
        return pltpu.make_async_remote_copy(
            src_ref=fin_out.at[t], dst_ref=out.at[slot], send_sem=fin_ss.at[t],
            recv_sem=fin_rs.at[slot], device_id=(4 * c + t, coil_to), device_id_type=MESH)

    for t in range(4):
        is_self = jnp.logical_and(4 * c + t == s, coil_to == c)

        @pl.when(jnp.logical_not(is_self))
        def _():
            final_copy(t).start()

        @pl.when(is_self)
        def _():
            copy = pltpu.make_async_copy(fin_out.at[t], out.at[slot], local_sem.at[1])
            copy.start()
            copy.wait()

    for t in range(4):
        is_self = jnp.logical_and(4 * c + t == s, coil_to == c)

        @pl.when(jnp.logical_not(is_self))
        def _():
            pltpu.make_async_remote_copy(
                src_ref=fin_out.at[t], dst_ref=out.at[t], send_sem=fin_ss.at[t],
                recv_sem=fin_rs.at[t], device_id=(4 * c + t, coil_to), device_id_type=MESH).wait()

    for part in range(2):
        for copy in sent[part]:
            copy.wait_send()


def local(
    noisy_image, noise_draw, block_routes, conv_in, bias_in, norm_gain, conv_mid, bias_mid, conv_out,
    coil_maps, kspace_data, sample_mask,
):
    taps_in = conv_in.astype(F32).reshape(3, 3, 128, 2).transpose(1, 3, 0, 2)
    w_in = jnp.pad(taps_in, ((0, 0), (0, 0), (0, 61), (0, 0))).reshape(384, 128)
    taps_mid = conv_mid.reshape(3, 3, 128, 128).transpose(0, 1, 3, 2).reshape(3, 384, 128)
    w_mid = jnp.concatenate(
        [jnp.pad(taps_mid, ((0, 1), (0, 0), (0, 0))), jnp.pad(taps_mid, ((1, 0), (0, 0), (0, 0)))], axis=2
    ).reshape(1536, 256)
    taps_out = conv_out.astype(F32).reshape(3, 3, 2, 128)[::-1].transpose(3, 1, 2, 0)
    w_out = jnp.pad(taps_out, ((0, 0), (0, 0), (0, 0), (0, 61))).reshape(128, 384)
    tables = [jnp.asarray(table) for table in dft_tables()]
    vmem = pl.BlockSpec(memory_space=pltpu.VMEM)
    hbm = pl.BlockSpec(memory_space=pl.ANY)
    prior, out = pl.pallas_call(
        kernel,
        out_shape=(
            jax.ShapeDtypeStruct((2, 1, R, N), F32),
            jax.ShapeDtypeStruct((4, 32, N), F32),
        ),
        in_specs=[vmem] * 10 + [hbm] * 8,
        out_specs=(vmem, vmem),
        scratch_shapes=[
            pltpu.VMEM((2, 2, NS, 10, N), F32),
            pltpu.VMEM((2, 2, NS, 10, N), F32),
            pltpu.VMEM((2 * N, 2 * N), BF16),
            pltpu.VMEM((2 * N, 2 * N), BF16),
            pltpu.VMEM((2 * N, 2 * N), BF16),
            pltpu.VMEM((2 * LP, 2 * LP), BF16),
            pltpu.VMEM((2 * LP, 2 * LP), BF16),
            pltpu.VMEM((2 * LP, 2 * LP), BF16),
            pltpu.VMEM((NS, 48, 2 * N), BF16),
            pltpu.VMEM((NS, 48, 2 * N), BF16),
            pltpu.VMEM((2, 16, N), F32),
            pltpu.VMEM((2, 16, N), F32),
            pltpu.VMEM((128, LP), F32),
            pltpu.VMEM((LP + 16, 128), F32),
            pltpu.VMEM((N, 384), BF16),
            pltpu.VMEM((N, 44 * LP), BF16),
            pltpu.VMEM((44, N, 128), BF16),
            pltpu.VMEM((N, 384), F32),
            pltpu.VMEM((2 * R, N), F32),
            pltpu.VMEM((NC, 2 * R, N), F32),
            pltpu.VMEM((2, N, LP), F32),
            pltpu.VMEM((2, 2 * R, LP), F32),
            pltpu.VMEM((2, 2 * R, LP), F32),
            pltpu.VMEM((2, 2 * R, LP), F32),
            pltpu.VMEM((4, LP, LP), F32),
            pltpu.VMEM((LP, LP), F32),
            pltpu.VMEM((2 * N, 2 * LP), F32),
            pltpu.VMEM((N, LP), F32),
            pltpu.VMEM((2, N, 2 * LP), F32),
            pltpu.VMEM((2, 2, N, LP), F32),
            pltpu.VMEM((2, N, LP), F32),
            pltpu.VMEM((2 * N, 2 * LP), BF16),
            pltpu.VMEM((2 * N, 2 * LP), BF16),
            pltpu.VMEM((2, NC, 2 * R, N), BF16),
            pltpu.VMEM((2, NC, 2 * R, N), BF16),
            pltpu.VMEM((2 * R, N), BF16),
            pltpu.VMEM((NC, 2 * R, N), BF16),
            pltpu.VMEM((4, 32, N), F32),
            pltpu.SemaphoreType.DMA((8,)),
            pltpu.SemaphoreType.DMA((2,)),
            pltpu.SemaphoreType.DMA((2,)),
            pltpu.SemaphoreType.DMA((2, NS - 1)),
            pltpu.SemaphoreType.DMA((2, NS - 1)),
            pltpu.SemaphoreType.DMA((NC - 1,)),
            pltpu.SemaphoreType.DMA((NC - 1,)),
            pltpu.SemaphoreType.DMA((2, 2)),
            pltpu.SemaphoreType.DMA((2, 2)),
            pltpu.SemaphoreType.DMA((2, NC - 1)),
            pltpu.SemaphoreType.DMA((2, NC - 1)),
            pltpu.SemaphoreType.DMA((NC - 1,)),
            pltpu.SemaphoreType.DMA((NC - 1,)),
            pltpu.SemaphoreType.DMA((4,)),
            pltpu.SemaphoreType.DMA((4,)),
            pltpu.SemaphoreType.DMA((2,)),
        ],
        compiler_params=pltpu.CompilerParams(
            collective_id=0, has_side_effects=True, vmem_limit_bytes=58 * 2**20
        ),
    )(
        noisy_image, noise_draw, block_routes, w_in, bias_in.reshape(1, 128), norm_gain.reshape(1, 128),
        w_mid, bias_mid.reshape(1, 128), w_out, sample_mask, coil_maps, kspace_data, *tables,
    )
    refined = out.reshape(4, 2, 16, N)[:, :, :10].transpose(1, 0, 3, 2)
    return prior, refined


def solution(mesh):
    return jax.shard_map(
        local,
        mesh=mesh,
        in_specs=(
            P(None, "slab", "coil", None),
            P(None, "slab", "coil", None),
            P("slab", None),
            P(), P(), P(), P(), P(), P(),
            P(None, "coil", None, "slab", None),
            P(None, "coil", None, "slab", None),
            P("slab", None),
        ),
        out_specs=(P(None, "slab", "coil", None), P(None, "coil", None, "slab")),
        check_vma=False,
    )
```

time: 663 us -> 129 us (0.19); the launches traced: 651 us -> 129 us
  waiting for transfers between devices: 275 us -> 0 us
  Pallas kernels: 0 us -> 114 us
  matrix products: 98.4 us -> 0 us
  local copies, waits for them, and re-layouts: 106 us -> 11.8 us
  blocking collectives: 60.8 us -> 0 us
  starting transfers between devices: 44.3 us -> 0 us
  other arithmetic: 46 us -> 2.37 us
  between operations: 15.3 us -> 0.66 us
    all_to_all x6 -> x0, waiting for transfers between devices: 151 us -> none  [the longest x2 114 us: local(): lax.all_to_all(returned, 'slab', split_axis=0, concat_axis=1, tiled=True)]
    psum x2 -> x0, waiting for transfers between devices: 124 us -> none  [local(): lax.psum(conjugate_sum(sens_maps, normal_returned, coils_here), 'coil')]
    pallas_call x0 -> x1, Pallas kernels: none -> 114 us  [local(): pl.pallas_call(kernel, out_shape=(jax.ShapeDtypeStruct((2, 1, R, N), F32)...]
    dot_general x29 -> x0, matrix products: 98.4 us -> none  [the longest x4 33.4 us: along_second(): sine_part = jnp.einsum('kh,whm->wkm', tables[1], paired, precision=HIGHEST)]
    all_to_all x1 -> x0, blocking collectives: 43.7 us -> none  [local(): lax.all_to_all(spectra.astype(jnp.bfloat16), 'slab', split_axis=1, concat...]
    all_to_all x6 -> x0, starting transfers between devices: 39.5 us -> none  [the longest x1 10.9 us: local(): lax.all_to_all(prior_step, 'slab', split_axis=3, concat_axis=1, tiled=True)]
    all_to_all x9 -> x0, local copies, waits for them, and re-layouts: 21.9 us -> none  [the longest x4 13 us: local(): lax.all_to_all(returned, 'slab', split_axis=0, concat_axis=1, tiled=True)]
    another operation x15 -> x0, local copies, waits for them, and re-layouts: 19.8 us -> none  [the longest x4 9.9 us: times_maps(): tiled_imag = jnp.tile(volume[..., slab_count:], (1, 1, coils_here))]
  transfers between devices with their start and end apart: 10 -> 0, of which waited for: 8 -> 0; matrix products, arithmetic and copies ran while one was open for 4% -> 0% of each run, Pallas kernels for 0% -> 0%
where the time goes in v1:
time: 129 us
  Pallas kernels  114 us (88%)
  local copies, waits for them, and re-layouts  11.8 us (9%)
  other arithmetic  2.37 us (2%)
    pallas_call x1, Pallas kernels, local(): pl.pallas_call(kernel, out_shape=(jax.ShapeDtypeStruct((2, 1, R, N), F32)...  114 us
    unnamed x9, local copies, waits for them, and re-layouts  8.93 us

profile of v1, /device:TPU:31, one launch (start us, length us, event | category | flops | bytes accessed | tf_op | source)
XLA Modules:
  0.0 128.9 jit_solution(13089809983723644055)
XLA Ops:
  0.6 0.0 copy-start
  0.6 0.8 copy.44
  1.5 0.7 convert.7
  2.2 0.7 bitcast_convert_fusion.w_in
  2.9 0.8 copy.35.w_out
  3.8 1.2 copy.33
  4.9 1.0 fusion.2
  5.9 0.0 copy-done
  5.9 0.0 copy-start.1
  5.9 2.8 %copy.36.maps_hbm = f32[2,2,32,10,320]{4,3,2,1,0:T(8,128)} copy(f32[2,2,32,10,320]{4,2,3,1,0:T(8,128)S(1)} %copy-done) | data formatting | bytes 3276800 | tf_op args[9]
  8.7 0.0 copy-done.1
  8.7 2.9 %copy.37.kdata_hbm = f32[2,2,32,10,320]{4,3,2,1,0:T(8,128)} copy(f32[2,2,32,10,320]{4,2,3,1,0:T(8,128)S(1)} %copy-done.1) | data formatting | bytes 3276800 | tf_op args[10]
  11.6 114.1 %shard_map.185 = (f32[2,1,40,320]{3,2,1,0:T(8,128)}, f32[4,32,320]{2,1,0:T(8,128)}) custom-call(f32[2,1,40,320]{3,2,1,0:T(8,128)} %noisy.1, f32[2,1,40,320]{3,2,1,0:T(8,128)} %noise.1, s32[1,40]{1,0:T(1,128)} %routes.1, f32[384,128]{1,0:T(8,128)} %bitcast_convert_fusion.w_in, f32[1,128]{1,0:T(1,128)} %bitcast.34, f32[1,128]{1,0:T(1,128)} %bitcast.35, ...), custom_call_target="tpu_custom_call" | custom-call | tf_op jit(solution)/shard_map/pallas_call | solution.py:442
  125.7 1.7 %copy.43 = f32[4,2,10,320]{3,0,2,1:T(4,128)} copy(f32[4,2,10,320]{3,2,1,0:T(8,128)} %bitcast.29) | data formatting | bytes 204800
  127.4 1.6 %copy.46 = f32[2,1,40,320]{3,2,1,0:T(8,128)} copy(f32[2,1,40,320]{3,2,1,0:T(8,128)} %get-tuple-element.8) | data formatting | bytes 204800
  (4 shorter events, 0.0 us)
Async XLA Ops:
  0.6 5.3 %copy-start = (f32[2,2,32,10,320]{4,2,3,1,0:T(8,128)S(1)}, f32[2,2,32,10,320]{4,2,3,1,0:T(8,128)}, u32[]{:S(2)}) copy-start(f32[2,2,32,10,320]{4,2,3,1,0:T(8,128)} %param.27) | copy-start | bytes 4915204
  5.9 2.8 %copy-start.1 = (f32[2,2,32,10,320]{4,2,3,1,0:T(8,128)S(1)}, f32[2,2,32,10,320]{4,2,3,1,0:T(8,128)}, u32[]{:S(2)}) copy-start(f32[2,2,32,10,320]{4,2,3,1,0:T(8,128)} %param.28) | copy-start | bytes 4915204

commit v2 on v1

v2 whole, which is shorter than its diff:
```python
import functools
import math

import jax
import jax.numpy as jnp
import numpy as np
from jax import lax
from jax.experimental import pallas as pl
from jax.experimental.pallas import tpu as pltpu
from jax.sharding import PartitionSpec as P

NS, NC, NZ, NY = 32, 8, 8, 4
N = 320
LP = 384
R = 40
STEP_VARIANCE = 1.0 - 0.8 * 0.8
STEP_SCALE = math.sqrt(STEP_VARIANCE)
STEP_SIZE = 0.4
PENALTY = 0.5
SHRINK = 0.3
EPSILON = 1e-05
F32, BF16 = jnp.float32, jnp.bfloat16
MESH = pl.DeviceIdType.MESH
ROWS = 104


def dft_tables():
    index = np.arange(N)
    angle = (index[:, None] * index[None, :] % N) * (2.0 * math.pi / N)
    cosine, sine = np.cos(angle) / math.sqrt(N), np.sin(angle) / math.sqrt(N)

    def left(sign):
        return np.block([[cosine, sign * sine], [-sign * sine, cosine]])

    def right(sign):
        table = np.zeros((2 * LP, 2 * LP))
        table[:N, :N] = table[LP : LP + N, LP : LP + N] = cosine
        table[:N, LP : LP + N] = -sign * sine
        table[LP : LP + N, :N] = sign * sine
        return table

    def split(table):
        import ml_dtypes

        high = table.astype(ml_dtypes.bfloat16)
        return high, (table - high.astype(np.float64)).astype(ml_dtypes.bfloat16)

    left_fwd, left_inv = split(left(1.0))[0], split(left(-1.0))
    right_fwd, right_inv = split(right(1.0))[0], split(right(-1.0))
    return left_fwd, left_inv[0], left_inv[1], right_fwd, right_inv[0], right_inv[1]


def silu(value):
    return value * (0.5 + 0.5 * jnp.tanh(0.5 * value))


def mm(a, b):
    return jnp.dot(a, b, preferred_element_type=F32)


def split_f32(value):
    high = value.astype(BF16)
    return high, (value - high.astype(F32)).astype(BF16)


def kernel(
    noisy, noise, routes, conv_in, b_in, gain, conv_mid, b_mid, conv_out, mask_in,
    maps_hbm, kdata_hbm, lf_hbm, li_hbm, lil_hbm, rf_hbm, ri_hbm, ril_hbm,
    prior, out,
    maps, kdata, lf, li, lil, rf, rinv, ril,
    w_in, w_mid, w_out, w_rows, stage, msg, got, halo_out, halo_in, x_nat, x_t, x3, act3, first, acc,
    ag_out, ag_in, own_out, own_in, v, zex_out, zex_in,
    kn, mk_out, mk_in, mask_t, kt, gadj, sens, adj,
    stage_f, stage_b, rs_out, rs_in, fin_out, fin_in,
    load_sem, halo_ss, halo_rs, a_ss, a_rs, own_ss, own_rs, z_ss, z_rs, mk_ss, mk_rs,
    rs_ss, rs_rs, ag_ss, ag_rs, fin_ss, fin_rs, local_sem,
):
    s, c = lax.axis_index("slab"), lax.axis_index("coil")
    z, y = s // NY, lax.rem(s, NY)
    loads = [
        pltpu.make_async_copy(src, dst, load_sem.at[i])
        for i, (src, dst) in enumerate(
            [(kdata_hbm, kdata), (maps_hbm, maps), (lf_hbm, lf), (li_hbm, li), (lil_hbm, lil),
             (rf_hbm, rf), (ri_hbm, rinv), (ril_hbm, ril)]
        )
    ]
    for load in loads:
        load.start()

    barrier = pltpu.get_barrier_semaphore()
    coil_peers = [lax.rem(c + k, NC) for k in range(1, NC)]
    def slab_to(offset):
        return lax.rem(z + offset // NY, NZ) * NY + lax.rem(y + lax.rem(offset, NY), NY)

    for peer in coil_peers:
        pl.semaphore_signal(barrier, inc=1, device_id=(s, peer), device_id_type=MESH)

    def greet(i, carry):
        pl.semaphore_signal(barrier, inc=1, device_id=(slab_to(i + 1), c), device_id_type=MESH)
        return carry

    lax.fori_loop(0, NS - 1, greet, 0)

    x_nat[...] = jnp.zeros_like(x_nat)
    for ch in range(2):
        rows = noisy[ch, 0].astype(BF16).astype(F32)
        x_nat[ch * 64 + 3 : ch * 64 + 43, 0:N] = rows
        halo_out[0, ch * 8 : ch * 8 + 3, :] = rows[0:3]
        halo_out[1, ch * 8 : ch * 8 + 3, :] = rows[R - 3 : R]

    def beside(real, imag):
        return jnp.concatenate(
            [real[:, 0:256], imag[:, 0:256], jnp.concatenate([real[:, 256:N], imag[:, 256:N]], axis=1)], axis=1
        )

    mask_f = jnp.concatenate([mask_in[...].astype(F32), jnp.zeros((10, LP - N), F32)], axis=1)
    mask_f = pltpu.roll(mask_f, lax.rem(LP - R * c, LP), 1)[:, 0:128]
    lane10 = lax.broadcasted_iota(jnp.int32, (4, 128), 1)
    mask_last = jnp.concatenate([mask_f[8:10], jnp.zeros((2, 128), F32)], axis=0)
    mask_rows = jnp.where(
        lane10 < R, mask_f[0:4],
        jnp.where(lane10 < 2 * R, pltpu.roll(mask_f[4:8], R, 1), pltpu.roll(mask_last, 2 * R, 1)))
    for row in range(4):
        stage[pl.ds(100 + row, NS, stride=ROWS), :] = jnp.broadcast_to(mask_rows[row : row + 1], (NS, 128))

    def pack(part, source):
        loads[part].wait()
        for j in range(2):
            for i in range(10):
                both = beside(source[0, j, i], source[1, j, i])
                for tile in range(5):
                    stage[pl.ds(20 * tile + 10 * j + i, NS, stride=ROWS), :] = both[:, tile * 128 : tile * 128 + 128]

        def narrow(dest, carry):
            msg[part, dest] = stage[pl.ds(pl.multiple_of(dest * ROWS, 8), ROWS), :].astype(BF16)
            return carry

        lax.fori_loop(0, NS, narrow, 0)

    pack(0, kdata)
    pack(1, maps)

    w_in[...] = jnp.zeros_like(w_in)
    w_mid[...] = jnp.zeros_like(w_mid)
    w_rows[...] = jnp.zeros_like(w_rows)
    for a in range(3):
        for b in range(3):
            taps = conv_in[3 * a + b].astype(F32)
            outs = conv_out[3 * a + b].astype(F32)
            for ch in range(2):
                w_in[b * 128 + ch * 64 + a : b * 128 + ch * 64 + a + 1, :] = taps[ch : ch + 1]
                w_rows[b, ch * 64 + 2 - a : ch * 64 + 3 - a, :] = outs[ch : ch + 1]
            middle = conv_mid[3 * a + b].astype(F32).T.astype(BF16)
            for q in range(2):
                at = ((a + q) * 3 + b) * 128
                w_mid[at : at + 128, q * 128 : q * 128 + 128] = middle
    for b in range(3):
        w_out[:, b * 128 : b * 128 + 128] = w_rows[b].T

    pl.semaphore_wait(barrier, NC - 1 + NS - 1)

    up, down = lax.rem(c + NC - 1, NC), lax.rem(c + 1, NC)
    halo = []
    for side, peer in ((0, up), (1, down)):
        copy = pltpu.make_async_remote_copy(
            src_ref=halo_out.at[side], dst_ref=halo_in.at[side], send_sem=halo_ss.at[side],
            recv_sem=halo_rs.at[side], device_id=(s, peer), device_id_type=MESH)
        copy.start()
        halo.append(copy)

    def message(part, offset):
        peer = slab_to(offset)
        return pltpu.make_async_remote_copy(
            src_ref=msg.at[part, peer], dst_ref=got.at[part, s], send_sem=a_ss.at[part, offset - 1],
            recv_sem=a_rs.at[part, offset - 1], device_id=(peer, c), device_id_type=MESH)

    for part in range(2):

        def send(i, carry):
            message(part, i + 1).start()
            return carry

        lax.fori_loop(0, NS - 1, send, 0)
    own_copies = [pltpu.make_async_copy(msg.at[part, s], got.at[part, s], local_sem.at[part]) for part in range(2)]
    for copy in own_copies:
        copy.start()

    x_t[0:8, :] = jnp.zeros((8, 128), F32)

    def build_x3():
        x_t[8 : 8 + LP, :] = x_nat[...].T
        for b in range(3):
            x3[:, b * 128 : b * 128 + 128] = x_t[7 + b : 7 + b + N, :].astype(BF16)

    build_x3()

    column = lax.broadcasted_iota(jnp.int32, (N, 128), 0)

    def shifted(value, offset):
        if offset == 0:
            return value
        if offset < 0:
            return jnp.where(column == 0, 0.0, pltpu.roll(value, 1, 0))
        return jnp.where(column == N - 1, 0.0, pltpu.roll(value, N - 1, 0))

    def inside(row):
        return jnp.where(jnp.logical_and(row >= 0, row < N), 1.0, 0.0).astype(F32)

    def first_pair(pair, carry):
        q = 2 * pair
        weights = jnp.concatenate(
            [pltpu.roll(w_in[...], q, 0), pltpu.roll(w_in[...], q + 1, 0)], axis=1).astype(BF16)
        both = mm(x3[...], weights)
        for half in range(2):
            state = (both[:, half * 128 : half * 128 + 128] + b_in[...]).astype(BF16)
            first[q + half] = state
            state = state.astype(F32)
            scale = lax.rsqrt(jnp.mean(state * state, axis=-1, keepdims=True) + EPSILON)
            active = silu(state * scale * gain[...]) * inside(c * R - 2 + q + half)
            for b in range(3):
                at = pl.multiple_of((q + half) * LP + b * 128, 128)
                act3[:, pl.ds(at, 128)] = shifted(active, b - 1).astype(BF16)
        return carry

    lax.fori_loop(2, 20, first_pair, 0)
    for copy in halo:
        copy.wait()
    for ch in range(2):
        above = jnp.where(c > 0, halo_in[1, ch * 8 : ch * 8 + 3, :], 0.0)
        below = jnp.where(c < NC - 1, halo_in[0, ch * 8 : ch * 8 + 3, :], 0.0)
        x_nat[ch * 64 : ch * 64 + 3, 0:N] = above
        x_nat[ch * 64 + 43 : ch * 64 + 46, 0:N] = below
    build_x3()
    lax.fori_loop(0, 2, first_pair, 0)
    lax.fori_loop(20, 22, first_pair, 0)

    acc[...] = jnp.zeros_like(acc)

    def second_pair(pair, carry):
        p = 2 * pair
        both = mm(act3[:, pl.ds(pl.multiple_of(p * LP, 128), 4 * LP)], w_mid[...])
        halves, weights = [], []
        for half in range(2):
            second = first[p + half + 1].astype(F32) + both[:, half * 128 : half * 128 + 128] + b_mid[...]
            second = second.astype(BF16).astype(F32)
            halves.append((silu(second) * inside(c * R - 1 + p + half)).astype(BF16))
            weights.append(jnp.concatenate(
                [pltpu.roll(w_out[:, b * 128 : b * 128 + 128], lax.rem(p + half + 126, 128), 1) for b in range(3)],
                axis=1))
        acc[...] += mm(jnp.concatenate(halves, axis=1), jnp.concatenate(weights, axis=0).astype(BF16))
        return carry

    lax.fori_loop(0, 21, second_pair, 0)

    score_t = shifted(acc[:, 0:128], -1) + acc[:, 128:256] + shifted(acc[:, 256:384], 1)
    x_t[0:N, :] = score_t
    score = x_t[0:LP, :].T
    block = lax.broadcasted_iota(jnp.int32, (R, 40), 1)
    block_of_row = c * 5 + lax.broadcasted_iota(jnp.int32, (R, 40), 0) // 8
    routed = jnp.where(routes[...] >= 0, 1.0, 0.0).astype(F32)
    keep = jnp.sum(jnp.where(block == block_of_row, jnp.broadcast_to(routed, (R, 40)), 0.0), axis=1, keepdims=True)
    stepped_parts = []
    for ch in range(2):
        value = score[ch * 64 : ch * 64 + R, 0:N].astype(BF16).astype(F32) * keep
        stepped = noisy[ch, 0] + STEP_VARIANCE * value + STEP_SCALE * noise[ch, 0]
        prior[ch, 0] = stepped
        x_nat[ch * 64 : ch * 64 + R, 0:N] = stepped
        stepped_parts.append(stepped)
    ag_out[0] = beside(stepped_parts[0], stepped_parts[1]).astype(BF16)

    def to_coil(src_of, dst, send_sems, recv_sems):
        copies = []
        for i, peer in enumerate(coil_peers):
            copy = pltpu.make_async_remote_copy(
                src_ref=src_of(peer), dst_ref=dst.at[c], send_sem=send_sems.at[i],
                recv_sem=recv_sems.at[i], device_id=(s, peer), device_id_type=MESH)
            copy.start()
            copies.append(copy)
        return copies

    gathered = to_coil(lambda peer: ag_out.at[0], ag_in.at[0], ag_ss.at[0], ag_rs.at[0])
    ag_in[0, c] = ag_out[0]
    own_out[...] = x_nat[...].T[0:N].reshape(NC, R, 128)
    chunked = to_coil(lambda peer: own_out.at[peer], own_in, own_ss, own_rs)
    own_in[c] = own_out[c]

    def to_neighbours(number):
        copies = []
        for side, peer in ((0, lax.rem(s + NS - 1, NS)), (1, lax.rem(s + 1, NS))):
            copy = pltpu.make_async_remote_copy(
                src_ref=zex_out.at[number], dst_ref=zex_in.at[number, side], send_sem=z_ss.at[number, side],
                recv_sem=z_rs.at[number, side], device_id=(peer, c), device_id_type=MESH)
            copy.start()
            copies.append(copy)
        return copies

    lane = lax.broadcasted_iota(jnp.int32, (R, 128), 1)
    lanes = lax.broadcasted_iota(jnp.int32, (R, LP), 1)

    def apart(tiles):
        zero = jnp.zeros_like(tiles[4])
        real_tail = jnp.where(lane < 64, tiles[4], zero)
        imag_tail = jnp.where(lane < 64, pltpu.roll(tiles[4], 64, 1), zero)
        return (jnp.concatenate([tiles[0], tiles[1], real_tail], axis=1),
                jnp.concatenate([tiles[2], tiles[3], imag_tail], axis=1))

    def apart_rows(rows):
        rows = rows.astype(F32)
        return apart([rows[:, k * 128 : k * 128 + 128] for k in range(5)])

    for copy in chunked:
        copy.wait()
    state = []
    for ch in range(2):
        total = jnp.zeros((R, LP), F32)
        for peer in range(NC):
            piece = own_in[peer]
            piece = jnp.concatenate([piece if ch == 0 else pltpu.roll(piece, 64, 1)] + [jnp.zeros((R, 256), F32)], axis=1)
            piece = piece if peer == 0 else pltpu.roll(piece, R * peer, 1)
            total = jnp.where(jnp.logical_and(lanes >= R * peer, lanes < R * peer + R), piece, total)
        state.append(total)
        zex_out[0, ch * R : ch * R + R, :] = total
    neighbours = to_neighbours(0)
    for copy in gathered:
        copy.wait()
    kn[...] = jnp.zeros_like(kn)
    for peer in range(NC):
        real, imag = apart_rows(ag_in[0, peer])
        kn[0, peer * R : peer * R + R, :] = real
        kn[1, peer * R : peer * R + R, :] = imag
    for ch in range(2):
        v[ch] = kn[ch].T[0:N, :]

    def regular(state, received, clip):
        result = []
        for ch in range(2):
            behind = received[1, ch * R : ch * R + R, :]
            ahead = received[0, ch * R : ch * R + R, :]
            low, high = state[ch] - behind, ahead - state[ch]
            if clip:
                low, high = 2.0 * jnp.clip(low, -SHRINK, SHRINK), 2.0 * jnp.clip(high, -SHRINK, SHRINK)
            result.append(jnp.where(s > 0, low, 0.0) - jnp.where(s < NS - 1, high, 0.0))
        return result

    mask_t[...] = jnp.zeros_like(mask_t)
    kn[...] = jnp.zeros_like(kn)

    def arrived(part, group_offset):
        for dy in range(NY):
            message(part, group_offset * NY + dy).wait_recv()

    def unpack(part, group, store):
        rows = [got[part, group * NY + i].astype(F32) for i in range(NY)]
        at = pl.multiple_of(group * R, 8)
        for j in range(2):
            tiles = [
                jnp.concatenate([rows[i][20 * k + 10 * j : 20 * k + 10 * j + 10] for i in range(NY)], axis=0)
                for k in range(5)
            ]
            store(j, at, apart(tiles))
        return rows, at

    def store_k(j, at, pair):
        kn[2 * j, pl.ds(at, R), :] = pair[0]
        kn[2 * j + 1, pl.ds(at, R), :] = pair[1]

    def unpack_k(group):
        rows, at = unpack(0, group, store_k)
        marks = []
        for i in range(NY):
            part = rows[i][100:104]
            marks += [part, pltpu.roll(part, 128 - R, 1), pltpu.roll(part, 128 - 2 * R, 1)[0:2]]
        x_t[pl.ds(at, R), :] = jnp.concatenate(marks, axis=0)

    def first_group(part):
        own_copies[part].wait()
        for dy in range(1, NY):
            message(part, dy).wait_recv()

    first_group(0)
    unpack_k(z)

    def next_k(dz, carry):
        arrived(0, dz)
        unpack_k(lax.rem(z + NZ - dz, NZ))
        return carry

    lax.fori_loop(1, NZ, next_k, 0)
    mk_out[...] = x_t[0:LP, :].T[0:R, 0:N].astype(BF16)
    masks = to_coil(lambda peer: mk_out, mk_in, mk_ss, mk_rs)
    mk_in[c] = mk_out[...]
    for j in range(2):
        for ch in range(2):
            kt[ch * N : ch * N + N, j * LP : j * LP + LP] = kn[2 * j + ch].T[0:N, :]
    for copy in masks:
        copy.wait()
    for peer in range(NC):
        mask_t[peer * R : peer * R + R, 0:N] = mk_in[peer].astype(F32)
    for ch in range(2):
        for j in range(2):
            kt[ch * N : ch * N + N, j * LP : j * LP + LP] *= mask_t[...]
    for load in loads[2:]:
        load.wait()
    high, low = split_f32(kt[...])
    kt[...] = mm(li[...], high) + mm(li[...], low) + mm(lil[...], high)
    for j in range(2):
        columns = jnp.concatenate(
            [kt[0:N, j * LP : j * LP + LP], kt[N : 2 * N, j * LP : j * LP + LP]], axis=1)
        high, low = split_f32(columns)
        gadj[j] = mm(high, rinv[...]) + mm(low, rinv[...]) + mm(high, ril[...])

    def store_maps(j, at, pair):
        sens[j, 0, pl.ds(at, R), :] = pair[0]
        sens[j, 1, pl.ds(at, R), :] = pair[1]

    first_group(1)
    unpack(1, z, store_maps)

    def next_maps(dz, carry):
        arrived(1, dz)
        unpack(1, lax.rem(z + NZ - dz, NZ), store_maps)
        return carry

    lax.fori_loop(1, NZ, next_maps, 0)

    def conjugate_sum(rows, images):
        real, imag = None, None
        for j in range(2):
            a, b = images[j][:, 0:LP], images[j][:, LP : 2 * LP]
            re = sens[j, 0, rows] * a + sens[j, 1, rows] * b
            im = sens[j, 0, rows] * b - sens[j, 1, rows] * a
            real, imag = (re, im) if real is None else (real + re, imag + im)
        return real, imag

    adj[0], adj[1] = conjugate_sum(pl.ds(0, N), [gadj[0], gadj[1]])

    def forward_rows(at, vr, vi):
        rows = pl.ds(at, R)
        for j in range(2):
            mr, mi = sens[j, 0, rows], sens[j, 1, rows]
            both = mm(jnp.concatenate([mr * vr - mi * vi, mr * vi + mi * vr], axis=1).astype(BF16), rf[...])
            for ch in range(2):
                part = both[:, ch * LP : ch * LP + LP]
                stage_f[pl.ds(ch * N + at, R), j * LP : j * LP + LP] = part

    def reduce_to(step, peer):
        rows = pl.ds(pl.multiple_of(peer * R, 8), R)
        images = []
        for j in range(2):
            columns = jnp.concatenate(
                [stage_f[rows, j * LP : j * LP + LP],
                 stage_f[pl.ds(pl.multiple_of(N + peer * R, 8), R), j * LP : j * LP + LP]], axis=1)
            images.append(mm(columns.astype(BF16), rinv[...]))
        real, imag = conjugate_sum(rows, images)
        rs_out[step, peer] = beside((real - adj[0, rows])[:, 0:N], (imag - adj[1, rows])[:, 0:N]).astype(BF16)

    for step in range(2):
        if step == 0:
            for peer in range(NC):
                forward_rows(peer * R, v[0, peer * R : peer * R + R, :], v[1, peer * R : peer * R + R, :])
        else:
            forward_rows(pl.multiple_of(c * R, 8), *apart_rows(ag_out[1]))
            for i, copy in enumerate(regathered):
                copy.wait_recv()
                sender = lax.rem(c + NC - 1 - i, NC)
                forward_rows(pl.multiple_of(sender * R, 8), *apart_rows(ag_in[1, sender]))
        spectrum = mm(lf[...], stage_f[...].astype(BF16))
        for ch in range(2):
            for j in range(2):
                stage_b[ch * N : ch * N + N, j * LP : j * LP + LP] = (
                    spectrum[ch * N : ch * N + N, j * LP : j * LP + LP] * mask_t[...]).astype(BF16)
        stage_f[...] = mm(li[...], stage_b[...])
        reduced = []
        for i, peer in enumerate(coil_peers):
            reduce_to(step, peer)
            copy = pltpu.make_async_remote_copy(
                src_ref=rs_out.at[step, peer], dst_ref=rs_in.at[step, c], send_sem=rs_ss.at[step, i],
                recv_sem=rs_rs.at[step, i], device_id=(s, peer), device_id_type=MESH)
            copy.start()
            reduced.append(copy)
        reduce_to(step, c)
        for copy in neighbours:
            copy.wait()
        smooth = regular(state, zex_in.at[step], step == 1)
        data = rs_out[step, c].astype(F32)
        for i, copy in enumerate(reduced):
            copy.wait()
            data = data + rs_in[step, lax.rem(c + NC - 1 - i, NC)].astype(F32)
        data = apart([data[:, k * 128 : k * 128 + 128] for k in range(5)])
        state = [state[ch] - STEP_SIZE * (data[ch] + PENALTY * smooth[ch]) for ch in range(2)]
        if step == 0:
            ag_out[1] = beside(state[0][:, 0:N], state[1][:, 0:N]).astype(BF16)
            regathered = to_coil(lambda peer: ag_out.at[1], ag_in.at[1], ag_ss.at[1], ag_rs.at[1])
            zex_out[1] = jnp.concatenate(state, axis=0)
            neighbours = to_neighbours(1)

    coil_to = s // NY
    slot = lax.rem(s, NY)
    result = beside(state[0][:, 0:N], state[1][:, 0:N])

    def final_copy(t, at):
        return pltpu.make_async_remote_copy(
            src_ref=fin_out.at[t], dst_ref=fin_in.at[at], send_sem=fin_ss.at[t],
            recv_sem=fin_rs.at[at], device_id=(4 * c + t, coil_to), device_id_type=MESH)

    for t in range(4):
        is_self = jnp.logical_and(4 * c + t == s, coil_to == c)
        for k in range(5):
            fin_out[t, 10 * k : 10 * k + 10, :] = result[10 * t : 10 * t + 10, k * 128 : k * 128 + 128]

        @pl.when(jnp.logical_not(is_self))
        def _():
            final_copy(t, slot).start()

        @pl.when(is_self)
        def _():
            copy = pltpu.make_async_copy(fin_out.at[t], fin_in.at[slot], local_sem.at[2])
            copy.start()
            copy.wait()

    for copy in regathered:
        copy.wait_send()
    for part in range(2):

        def sent(i, carry):
            message(part, i + 1).wait_send()
            return carry

        lax.fori_loop(0, NS - 1, sent, 0)

    for t in range(4):
        is_self = jnp.logical_and(4 * c + t == s, coil_to == c)

        @pl.when(jnp.logical_not(is_self))
        def _():
            final_copy(t, t).wait()

        rows = fin_in[t]
        tiles = [rows[10 * k : 10 * k + 10] for k in range(5)]
        tiles[4] = tiles[4][:, 0:64], tiles[4][:, 64:128]
        for ch in range(2):
            out[ch, :, t, :] = jnp.concatenate([tiles[2 * ch], tiles[2 * ch + 1], tiles[4][ch]], axis=1)


def local(
    noisy_image, noise_draw, block_routes, conv_in, bias_in, norm_gain, conv_mid, bias_mid, conv_out,
    coil_maps, kspace_data, sample_mask,
):
    tables = [jnp.asarray(table) for table in dft_tables()]
    vmem = pl.BlockSpec(memory_space=pltpu.VMEM)
    hbm = pl.BlockSpec(memory_space=pl.ANY)
    prior, out = pl.pallas_call(
        kernel,
        out_shape=(
            jax.ShapeDtypeStruct((2, 1, R, N), F32),
            jax.ShapeDtypeStruct((2, 10, 4, N), F32),
        ),
        in_specs=[vmem] * 10 + [hbm] * 8,
        out_specs=(vmem, vmem),
        scratch_shapes=[
            pltpu.VMEM((2, 2, 10, NS, N), F32),
            pltpu.VMEM((2, 2, 10, NS, N), F32),
            pltpu.VMEM((2 * N, 2 * N), BF16),
            pltpu.VMEM((2 * N, 2 * N), BF16),
            pltpu.VMEM((2 * N, 2 * N), BF16),
            pltpu.VMEM((2 * LP, 2 * LP), BF16),
            pltpu.VMEM((2 * LP, 2 * LP), BF16),
            pltpu.VMEM((2 * LP, 2 * LP), BF16),
            pltpu.VMEM((384, 128), F32),
            pltpu.VMEM((1536, 256), BF16),
            pltpu.VMEM((128, 384), F32),
            pltpu.VMEM((3, 128, 128), F32),
            pltpu.VMEM((NS * ROWS, 128), F32),
            pltpu.VMEM((2, NS, ROWS, 128), BF16),
            pltpu.VMEM((2, NS, ROWS, 128), BF16),
            pltpu.VMEM((2, 16, N), F32),
            pltpu.VMEM((2, 16, N), F32),
            pltpu.VMEM((128, LP), F32),
            pltpu.VMEM((LP + 16, 128), F32),
            pltpu.VMEM((N, 384), BF16),
            pltpu.VMEM((N, 44 * LP), BF16),
            pltpu.VMEM((44, N, 128), BF16),
            pltpu.VMEM((N, 384), F32),
            pltpu.VMEM((2, R, 2 * N), BF16),
            pltpu.VMEM((2, NC, R, 2 * N), BF16),
            pltpu.VMEM((NC, R, 128), F32),
            pltpu.VMEM((NC, R, 128), F32),
            pltpu.VMEM((2, N, LP), F32),
            pltpu.VMEM((2, 2 * R, LP), F32),
            pltpu.VMEM((2, 2, 2 * R, LP), F32),
            pltpu.VMEM((4, LP, LP), F32),
            pltpu.VMEM((R, N), BF16),
            pltpu.VMEM((NC, R, N), BF16),
            pltpu.VMEM((N, LP), F32),
            pltpu.VMEM((2 * N, 2 * LP), F32),
            pltpu.VMEM((2, N, 2 * LP), F32),
            pltpu.VMEM((2, 2, N, LP), F32),
            pltpu.VMEM((2, N, LP), F32),
            pltpu.VMEM((2 * N, 2 * LP), F32),
            pltpu.VMEM((2 * N, 2 * LP), BF16),
            pltpu.VMEM((2, NC, R, 2 * N), BF16),
            pltpu.VMEM((2, NC, R, 2 * N), BF16),
            pltpu.VMEM((4, 56, 128), F32),
            pltpu.VMEM((4, 56, 128), F32),
            pltpu.SemaphoreType.DMA((8,)),
            pltpu.SemaphoreType.DMA((2,)),
            pltpu.SemaphoreType.DMA((2,)),
            pltpu.SemaphoreType.DMA((2, NS - 1)),
            pltpu.SemaphoreType.DMA((2, NS - 1)),
            pltpu.SemaphoreType.DMA((NC - 1,)),
            pltpu.SemaphoreType.DMA((NC - 1,)),
            pltpu.SemaphoreType.DMA((2, 2)),
            pltpu.SemaphoreType.DMA((2, 2)),
            pltpu.SemaphoreType.DMA((NC - 1,)),
            pltpu.SemaphoreType.DMA((NC - 1,)),
            pltpu.SemaphoreType.DMA((2, NC - 1)),
            pltpu.SemaphoreType.DMA((2, NC - 1)),
            pltpu.SemaphoreType.DMA((2, NC - 1)),
            pltpu.SemaphoreType.DMA((2, NC - 1)),
            pltpu.SemaphoreType.DMA((4,)),
            pltpu.SemaphoreType.DMA((4,)),
            pltpu.SemaphoreType.DMA((3,)),
        ],
        compiler_params=pltpu.CompilerParams(
            collective_id=0, has_side_effects=True, vmem_limit_bytes=58 * 2**20
        ),
    )(
        noisy_image, noise_draw, block_routes, conv_in.transpose(0, 2, 1), bias_in.reshape(1, 128),
        norm_gain.reshape(1, 128), conv_mid, bias_mid.reshape(1, 128), conv_out, sample_mask,
        coil_maps.transpose(0, 1, 3, 2, 4), kspace_data.transpose(0, 1, 3, 2, 4), *tables,
    )
    refined = out.transpose(0, 2, 3, 1)
    return prior, refined


def solution(mesh):
    return jax.shard_map(
        local,
        mesh=mesh,
        in_specs=(
            P(None, "slab", "coil", None),
            P(None, "slab", "coil", None),
            P("slab", None),
            P(), P(), P(), P(), P(), P(),
            P(None, "coil", None, "slab", None),
            P(None, "coil", None, "slab", None),
            P("slab", None),
        ),
        out_specs=(P(None, "slab", "coil", None), P(None, "coil", None, "slab")),
        check_vma=False,
    )
```

time: 129 us -> 114 us (0.88)
  local copies, waits for them, and re-layouts: 11.8 us -> 3.12 us
  Pallas kernels: 114 us -> 109 us
  other arithmetic: 2.37 us -> 0 us
    unnamed x9 -> x2, local copies, waits for them, and re-layouts: 8.93 us -> 3.12 us
    pallas_call x1, Pallas kernels: 114 us -> 109 us  [local(): pl.pallas_call(kernel, out_shape=(jax.ShapeDtypeStruct((2, 1, R, N), F32)...]
    reshape x2 -> x0, local copies, waits for them, and re-layouts: 1.65 us -> none  [the longest x1 0.83 us: local(): taps_in = conv_in.astype(F32).reshape(3, 3, 128, 2).transpose(1, 3, 0, 2)]
    reshape x2 -> x0, other arithmetic: 1.41 us -> none  [the longest x1 0.72 us: local(): w_in = jnp.pad(taps_in, ((0, 0), (0, 0), (0, 61), (0, 0))).reshape(384, 128)]
where the time goes in v2:
time: 114 us; the launch traced here: 113 us
  Pallas kernels  109 us (96%)
  local copies, waits for them, and re-layouts  3.12 us (3%)
    pallas_call x1, Pallas kernels, local(): pl.pallas_call(kernel, out_shape=(jax.ShapeDtypeStruct((2, 1, R, N), F32)...  109 us
    unnamed x2, local copies, waits for them, and re-layouts  3.12 us

profile of v2, /device:TPU:31, one launch (start us, length us, event | category | flops | bytes accessed | tf_op | source)
XLA Modules:
  0.0 112.8 jit_solution(10825403816766402702)
XLA Ops:
  0.6 109.0 %shard_map.185 = (f32[2,1,40,320]{3,2,1,0:T(8,128)}, f32[2,10,4,320]{3,2,1,0:T(4,128)}) custom-call(f32[2,1,40,320]{3,2,1,0:T(8,128)} %noisy.1, f32[2,1,40,320]{3,2,1,0:T(8,128)} %noise.1, s32[1,40]{1,0:T(1,128)} %routes.1, bf16[9,2,128]{2,1,0:T(2,128)(2,1)} %bitcast.10, f32[1,128]{1,0:T(1,128)} %bitcast.11, f32[1,128]{1,0:T(1,128)} %bitcast.12, ...), custom_call_target="tpu_custom_call" | custom-call | tf_op jit(solution)/shard_map/pallas_call | solution.py:552
  109.7 1.6 %copy.22 = f32[2,1,40,320]{3,2,1,0:T(8,128)} copy(f32[2,1,40,320]{3,2,1,0:T(8,128)} %get-tuple-element.8) | data formatting | bytes 204800
  111.2 1.6 %copy.23 = f32[2,4,320,10]{2,1,3,0:T(4,128)} copy(f32[2,4,320,10]{2,1,3,0:T(4,128)} %bitcast.9) | data formatting | bytes 204800

commit v3 on v2

--- a/solution.py
+++ b/solution.py
@@ -308,6 +308,67 @@
         rows = rows.astype(F32)
         return apart([rows[:, k * 128 : k * 128 + 128] for k in range(5)])
 
+    def regular(state, received, clip):
+        result = []
+        for ch in range(2):
+            behind = received[1, ch * R : ch * R + R, :]
+            ahead = received[0, ch * R : ch * R + R, :]
+            low, high = state[ch] - behind, ahead - state[ch]
+            if clip:
+                low, high = 2.0 * jnp.clip(low, -SHRINK, SHRINK), 2.0 * jnp.clip(high, -SHRINK, SHRINK)
+            result.append(jnp.where(s > 0, low, 0.0) - jnp.where(s < NS - 1, high, 0.0))
+        return result
+
+    mask_t[...] = jnp.zeros_like(mask_t)
+    kn[...] = jnp.zeros_like(kn)
+
+    def arrived(part, group_offset):
+        for dy in range(NY):
+            message(part, group_offset * NY + dy).wait_recv()
+
+    def unpack(part, group, store):
+        rows = [got[part, group * NY + i].astype(F32) for i in range(NY)]
+        at = pl.multiple_of(group * R, 8)
+        for j in range(2):
+            tiles = [
+                jnp.concatenate([rows[i][20 * k + 10 * j : 20 * k + 10 * j + 10] for i in range(NY)], axis=0)
+                for k in range(5)
+            ]
+            store(j, at, apart(tiles))
+        return rows, at
+
+    def store_k(j, at, pair):
+        kn[2 * j, pl.ds(at, R), :] = pair[0]
+        kn[2 * j + 1, pl.ds(at, R), :] = pair[1]
+
+    def unpack_k(group):
+        rows, at = unpack(0, group, store_k)
+        marks = []
+        for i in range(NY):
+            part = rows[i][100:104]
+            marks += [part, pltpu.roll(part, 128 - R, 1), pltpu.roll(part, 128 - 2 * R, 1)[0:2]]
+        x_t[pl.ds(at, R), :] = jnp.concatenate(marks, axis=0)
+
+    def first_group(part):
+        own_copies[part].wait()
+        for dy in range(1, NY):
+            message(part, dy).wait_recv()
+
+    first_group(0)
+    unpack_k(z)
+
+    def next_k(dz, carry):
+        arrived(0, dz)
+        unpack_k(lax.rem(z + NZ - dz, NZ))
+        return carry
+
+    lax.fori_loop(1, NZ, next_k, 0)
+    mk_out[...] = x_t[0:LP, :].T[0:R, 0:N].astype(BF16)
+    masks = to_coil(lambda peer: mk_out, mk_in, mk_ss, mk_rs)
+    mk_in[c] = mk_out[...]
+    for j in range(2):
+        for ch in range(2):
+            kt[ch * N : ch * N + N, j * LP : j * LP + LP] = kn[2 * j + ch].T[0:N, :]
     for copy in chunked:
         copy.wait()
     state = []
@@ -323,7 +384,6 @@
     neighbours = to_neighbours(0)
     for copy in gathered:
         copy.wait()
-    kn[...] = jnp.zeros_like(kn)
     for peer in range(NC):
         real, imag = apart_rows(ag_in[0, peer])
         kn[0, peer * R : peer * R + R, :] = real
@@ -331,67 +391,6 @@
     for ch in range(2):
         v[ch] = kn[ch].T[0:N, :]
 
-    def regular(state, received, clip):
-        result = []
-        for ch in range(2):
-            behind = received[1, ch * R : ch * R + R, :]
-            ahead = received[0, ch * R : ch * R + R, :]
-            low, high = state[ch] - behind, ahead - state[ch]
-            if clip:
-                low, high = 2.0 * jnp.clip(low, -SHRINK, SHRINK), 2.0 * jnp.clip(high, -SHRINK, SHRINK)
-            result.append(jnp.where(s > 0, low, 0.0) - jnp.where(s < NS - 1, high, 0.0))
-        return result
-
-    mask_t[...] = jnp.zeros_like(mask_t)
-    kn[...] = jnp.zeros_like(kn)
-
-    def arrived(part, group_offset):
-        for dy in range(NY):
-            message(part, group_offset * NY + dy).wait_recv()
-
-    def unpack(part, group, store):
-        rows = [got[part, group * NY + i].astype(F32) for i in range(NY)]
-        at = pl.multiple_of(group * R, 8)
-        for j in range(2):
-            tiles = [
-                jnp.concatenate([rows[i][20 * k + 10 * j : 20 * k + 10 * j + 10] for i in range(NY)], axis=0)
-                for k in range(5)
-            ]
-            store(j, at, apart(tiles))
-        return rows, at
-
-    def store_k(j, at, pair):
-        kn[2 * j, pl.ds(at, R), :] = pair[0]
-        kn[2 * j + 1, pl.ds(at, R), :] = pair[1]
-
-    def unpack_k(group):
-        rows, at = unpack(0, group, store_k)
-        marks = []
-        for i in range(NY):
-            part = rows[i][100:104]
-            marks += [part, pltpu.roll(part, 128 - R, 1), pltpu.roll(part, 128 - 2 * R, 1)[0:2]]
-        x_t[pl.ds(at, R), :] = jnp.concatenate(marks, axis=0)
-
-    def first_group(part):
-        own_copies[part].wait()
-        for dy in range(1, NY):
-            message(part, dy).wait_recv()
-
-    first_group(0)
-    unpack_k(z)
-
-    def next_k(dz, carry):
-        arrived(0, dz)
-        unpack_k(lax.rem(z + NZ - dz, NZ))
-        return carry
-
-    lax.fori_loop(1, NZ, next_k, 0)
-    mk_out[...] = x_t[0:LP, :].T[0:R, 0:N].astype(BF16)
-    masks = to_coil(lambda peer: mk_out, mk_in, mk_ss, mk_rs)
-    mk_in[c] = mk_out[...]
-    for j in range(2):
-        for ch in range(2):
-            kt[ch * N : ch * N + N, j * LP : j * LP + LP] = kn[2 * j + ch].T[0:N, :]
     for copy in masks:
         copy.wait()
     for peer in range(NC):
@@ -540,6 +539,11 @@
         tiles[4] = tiles[4][:, 0:64], tiles[4][:, 64:128]
         for ch in range(2):
             out[ch, :, t, :] = jnp.concatenate([tiles[2 * ch], tiles[2 * ch + 1], tiles[4][ch]], axis=1)
+
+
+def hand_over(prior_in, out_in, prior, out):
+    prior[...] = prior_in[...]
+    out[...] = out_in[...]
 
 
 def local(
@@ -629,6 +633,12 @@
         norm_gain.reshape(1, 128), conv_mid, bias_mid.reshape(1, 128), conv_out, sample_mask,
         coil_maps.transpose(0, 1, 3, 2, 4), kspace_data.transpose(0, 1, 3, 2, 4), *tables,
     )
+    prior, out = pl.pallas_call(
+        hand_over,
+        out_shape=(jax.ShapeDtypeStruct(prior.shape, F32), jax.ShapeDtypeStruct(out.shape, F32)),
+        in_specs=[vmem, vmem],
+        out_specs=(vmem, vmem),
+    )(prior, out)
     refined = out.transpose(0, 2, 3, 1)
     return prior, refined
 

time: 114 us -> 108 us (0.947)
  local copies, waits for them, and re-layouts: 3.12 us -> 0 us
  Pallas kernels: 109 us -> 106 us
    pallas_call x1, Pallas kernels: 109 us -> 104 us  [local(): pl.pallas_call(kernel, out_shape=(jax.ShapeDtypeStruct((2, 1, R, N), F32)...]
    unnamed x2 -> x0, local copies, waits for them, and re-layouts: 3.12 us -> none
    pallas_call x0 -> x1, Pallas kernels: none -> 1.66 us  [local(): pl.pallas_call(hand_over, out_shape=(jax.ShapeDtypeStruct(prior.shape, F3...]
where the time goes in v3:
time: 108 us; the launch traced here: 107 us
  Pallas kernels  106 us (98%)
    pallas_call x1, Pallas kernels, local(): pl.pallas_call(kernel, out_shape=(jax.ShapeDtypeStruct((2, 1, R, N), F32)...  104 us

profile of v3, /device:TPU:31, one launch (start us, length us, event | category | flops | bytes accessed | tf_op | source)
XLA Modules:
  0.0 106.6 jit_solution(14246340317818925165)
XLA Ops:
  0.6 104.3 %shard_map.185 = (f32[2,1,40,320]{3,2,1,0:T(8,128)}, f32[2,10,4,320]{3,2,1,0:T(4,128)}) custom-call(f32[2,1,40,320]{3,2,1,0:T(8,128)} %noisy.1, f32[2,1,40,320]{3,2,1,0:T(8,128)} %noise.1, s32[1,40]{1,0:T(1,128)} %routes.1, bf16[9,2,128]{2,1,0:T(2,128)(2,1)} %bitcast.9, f32[1,128]{1,0:T(1,128)} %bitcast.10, f32[1,128]{1,0:T(1,128)} %bitcast.11, ...), custom_call_target="tpu_custom_call" | custom-call | tf_op jit(solution)/shard_map/pallas_call | solution.py:556
  104.9 1.7 %shard_map.186 = (f32[2,1,40,320]{3,2,1,0:T(8,128)}, f32[2,10,4,320]{3,2,1,0:T(4,128)}) custom-call(f32[2,1,40,320]{3,2,1,0:T(8,128)} %get-tuple-element.6.prior_in, f32[2,10,4,320]{3,2,1,0:T(4,128)} %get-tuple-element.7.out_in), custom_call_target="tpu_custom_call" | custom-call | tf_op jit(solution)/shard_map/pallas_call | solution.py:636
